TPU v7x, 128 devices: a whole 4x4x4 slice. The times are simulated.
128 devices in a mesh: cache: 32 (over x, y, core), item: 4 (over z).
Axes of the slice: x: 4, y: 4, z: 4, core: 2. Of those that a mesh axis runs over, the one named last changes fastest.
Arguments:
- cand_items: int32 [32, 1024], P('cache'), may hold values from 0 to 8191
- item_table: bfloat16 [8192, 1024], P('item'), may hold values from -6 to 6
- kv_cache: bfloat16 [2048, 128, 16, 128], P('cache', None, 'item'), may hold values from -6 to 6
- hist_blocks: int32 [32, 64], replicated, may hold values from 0 to 2047, as said below
- pattern: int32 [32, 4, 64], P('cache'), may hold values 0 or 1
- w_query: bfloat16 [1024, 1024], P(None, 'item'), may hold values from -0.1875 to 0.1875
- w_gate: bfloat16 [1024, 1024], replicated, may hold values from -0.1875 to 0.1875
- norm_gain: float32 [1024], replicated, may hold values from 0.1 to 1.9
- w_out: bfloat16 [1024, 1024], replicated, may hold values from -0.1875 to 0.1875
Outputs:
- layer_out: bfloat16 [32, 1024, 1024], P('cache', 'item')
Inputs may be any that keep to these rules, and one draw needn't show every extreme that they name: `hist_blocks`: entry b names a block held by index b // 64 of cache. The 64 blocks of one request are distinct, at most 4 of them are held by one index of cache, and every request has exactly 4 on some index.
All inputs are finite; a program needn't handle non-finite values. No bound on the sum of `pattern` on one device may be relied on, other than what follows from the above.
Results may differ from a plain program's by a relative error of at most 0.0046.
Values may be sent and summed in bfloat16 or wider, within the bound.
A program may use at most 128 MiB of HBM per device.

v0:
```python
import jax
import jax.numpy as jnp
from jax import lax
from jax.sharding import PartitionSpec as P

DH = 64
BLK = 128
SLOT = 4
CB = 256


norm_eps = 1e-05


def on_device(
    cand_items, item_table, kv_cache, hist_blocks, pattern, w_query, w_gate, norm_gain, w_out
):
    shard_pos = lax.axis_index("item")
    shard_count = lax.axis_size("item")
    device_here = lax.axis_index("cache")
    item_ids = cand_items[0]
    cand_count = item_ids.shape[0]
    width = w_gate.shape[0]
    table_rows = item_table.shape[0]
    local_ids = item_ids - shard_pos * table_rows
    inside = (local_ids >= 0) & (local_ids < table_rows)
    picked = jnp.take(item_table, jnp.clip(local_ids, 0, table_rows - 1), axis=0)
    term_rows = jnp.where(inside[:, None], picked, jnp.zeros((), picked.dtype))
    embedded = lax.psum(term_rows, "item").astype(jnp.float32).astype(jnp.bfloat16)
    head_width = w_query.shape[1]
    heads_here = head_width // DH
    queries = jax.nn.silu(jnp.dot(embedded, w_query, preferred_element_type=jnp.float32)).astype(
        jnp.bfloat16
    )
    queries = queries.reshape(cand_count // CB, CB, heads_here, DH)
    blocks_here = kv_cache.shape[0]
    list_len = hist_blocks.shape[1]
    owner_of = hist_blocks // blocks_here
    same_owner = owner_of[:, :, None] == owner_of[:, None, :]
    positions = jnp.arange(list_len)
    earlier = positions[None, :] < positions[:, None]
    slot_rank = jnp.sum(same_owner & earlier[None], axis=2)
    selected = (owner_of == device_here)[:, None, :] & (
        slot_rank[:, None, :] == jnp.arange(SLOT)[None, :, None]
    )
    local_block = jnp.sum(jnp.where(selected, hist_blocks[:, None, :] % blocks_here, 0), axis=2)
    filled = jnp.any(selected, axis=2)
    outgoing = jnp.take(kv_cache, local_block.reshape(-1), axis=0)
    outgoing = jnp.where(
        filled.reshape(-1)[:, None, None, None], outgoing, jnp.zeros((), outgoing.dtype)
    )
    outgoing = outgoing.reshape((owner_of.shape[0], SLOT) + kv_cache.shape[1:])
    received = lax.all_to_all(outgoing, "cache", split_axis=0, concat_axis=0, tiled=True)
    received = received.reshape((-1,) + kv_cache.shape[1:])
    my_owner = lax.dynamic_index_in_dim(owner_of, device_here, 0, keepdims=False)
    my_rank = lax.dynamic_index_in_dim(slot_rank, device_here, 0, keepdims=False)
    history = jnp.take(received, my_owner * SLOT + my_rank, axis=0)
    group_blocks = min(list_len, max(1, 4096 // BLK))
    group_count = list_len // group_blocks
    grouped = history.reshape(group_count, group_blocks * BLK, heads_here, 2 * DH)
    key_mask = jnp.repeat(pattern[0].astype(jnp.float32), BLK, axis=1)
    key_mask = key_mask.reshape(cand_count // CB, group_count, group_blocks * BLK)
    score_scale = DH ** (-0.5)

    def one_block(block_in):
        query_block, mask_row = block_in

        def over_group(running, group_in):
            kv_group, mask_part = group_in
            scores = (
                jnp.einsum(
                    "chd,khd->hck",
                    query_block,
                    kv_group[:, :, :DH],
                    preferred_element_type=jnp.float32,
                )
                * score_scale
            )
            weights = (jax.nn.silu(scores) * mask_part[None, None, :]).astype(jnp.bfloat16)
            return (
                running
                + jnp.einsum(
                    "hck,khd->chd", weights, kv_group[:, :, DH:], preferred_element_type=jnp.float32
                ),
                None,
            )

        running, _ = lax.scan(
            over_group, jnp.zeros((CB, heads_here, DH), jnp.float32), (grouped, mask_row)
        )
        return running

    attended = lax.map(one_block, (queries, key_mask)).reshape(cand_count, head_width)
    rows_per = cand_count // shard_count
    own_rows = lax.dynamic_slice_in_dim(embedded, shard_pos * rows_per, rows_per, 0)
    gate_cols = lax.dynamic_slice_in_dim(w_gate, shard_pos * head_width, head_width, 1)
    gate_act = jax.nn.silu(jnp.dot(embedded, gate_cols, preferred_element_type=jnp.float32))
    row_sums = lax.psum((jnp.sum(attended, axis=1), jnp.sum(attended * attended, axis=1)), "item")
    row_mean = row_sums[0] / width
    row_var = row_sums[1] / width - row_mean * row_mean
    gain_part = lax.dynamic_slice_in_dim(norm_gain, shard_pos * head_width, head_width, 0)
    normed = (attended - row_mean[:, None]) * lax.rsqrt(row_var + norm_eps)[:, None]
    hidden = (normed * gain_part[None, :] * gate_act).astype(jnp.bfloat16)
    out_part = lax.dynamic_slice_in_dim(w_out, shard_pos * head_width, head_width, 0)
    projected_rows = lax.psum_scatter(
        jnp.dot(hidden, out_part, preferred_element_type=jnp.float32),
        "item",
        scatter_dimension=0,
        tiled=True,
    )
    layer_out = (own_rows.astype(jnp.float32) + projected_rows).astype(jnp.bfloat16)
    return layer_out[None]


def solution(mesh):
    placed = (
        P("cache", None),
        P("item", None),
        P("cache", None, "item", None),
        P(),
        P("cache", None, None),
        P(None, "item"),
        P(),
        P(),
        P(),
    )
    return jax.shard_map(
        on_device, mesh=mesh, in_specs=placed, out_specs=P("cache", "item", None), check_vma=False
    )
```

profile of v0, /device:TPU:0, one launch (start us, length us, event | category | flops | bytes accessed | tf_op | source)
XLA Modules:
  0.0 560.1 jit_solution(11405423558608397342)
XLA Ops:
  6.6 0.9 add_select_fusion
  8.2 0.9 convert_reduce_fusion
  9.8 19.9 %gather_fusion.1 = bf16[128,128,4,128]{3,2,1,0:T(4,128)(2,1)} fusion(bf16[64,128,4,128]{3,2,1,0:T(4,128)(2,1)} %param.15, s32[1024]{0:T(1024)S(1)} %pad_clamp_fusion.1), kind=kCustom, calls=%fused_computation.1 | custom fusion | bytes 33554944 | tf_op jit(solution)/shard_map/jit(_take)/gather | solution.py:48
  29.7 15.3 %fusion.21 = bf16[32,4,128,4,128]{4,2,3,1,0:T(8,128)(2,1)} fusion(bf16[32,4,128,4,128]{4,3,2,1,0:T(4,128)(2,1)} %bitcast.82, pred[32,4]{1,0:T(8,128)(4,1)S(1)} %copy.30, pred[32,4]{1,0:T(8,128)(4,1)S(1)} %copy.29), kind=kLoop, calls=%fused_computation.23 | loop fusion | flops 16777216 | bytes 33554688 | tf_op jit(solution)/shard_map/jit(_where)/select_n | solution.py:49
  45.0 8.4 %all-to-all-start = ((bf16[32,4,128,4,128]{4,2,3,1,0:T(8,128)(2,1)}), bf16[32,4,128,4,128]{4,2,3,1,0:T(8,128)(2,1)}, u32[]{:S(2)}, u32[]{:S(2)}) async-start(bf16[32,4,128,4,128]{4,2,3,1,0:T(8,128)(2,1)} %fusion.21), calls=%async_computation | async-start | bytes 33554432 | tf_op jit(solution)/shard_map/all_to_all | solution.py:53
  53.5 8.7 %gather_fusion = bf16[1024,1024]{1,0:T(8,128)(2,1)} fusion(bf16[2048,1024]{1,0:T(8,128)(2,1)} %param.14, s32[1024]{0:T(1024)S(1)} %broadcast_clamp_fusion), kind=kCustom, calls=%fused_computation | custom fusion | bytes 4198400 | tf_op jit(solution)/shard_map/jit(_take)/gather | solution.py:27
  62.3 3.1 select_select_fusion
  67.9 1.4 dynamic_slice.38
  69.2 57.7 %all-reduce.3.cloned.1.call-done = bf16[1024,1024]{1,0:T(8,128)(2,1)} async-done(((bf16[1024,1024]{1,0:T(8,128)(2,1)}), bf16[1024,1024]{1,0:T(8,128)(2,1)}) %all-reduce.3.cloned.1.call-update) | async-done | bytes 2097168 | tf_op jit(solution)/shard_map/psum | solution.py:29
  126.9 3.2 multiply_convert_fusion.1
  130.1 2.7 reshape.210
  132.9 2.2 copy.34
  135.0 159.3 %all-to-all-done = bf16[32,4,128,4,128]{4,2,3,1,0:T(8,128)(2,1)} async-done(((bf16[32,4,128,4,128]{4,2,3,1,0:T(8,128)(2,1)}), bf16[32,4,128,4,128]{4,2,3,1,0:T(8,128)(2,1)}, u32[]{:S(2)}, u32[]{:S(2)}) %all-to-all-start) | async-done | bytes 16777248 | tf_op jit(solution)/shard_map/all_to_all | solution.py:53
  294.3 11.3 %gather_fusion.2 = bf16[64,128,4,128]{3,1,2,0:T(8,128)(2,1)} fusion(bf16[128,128,4,128]{3,1,2,0:T(8,128)(2,1)} %bitcast.9, s32[1024]{0:T(1024)S(1)} %pad_clamp_fusion), kind=kCustom, calls=%fused_computation.2 | custom fusion | bytes 16777472 | tf_op jit(solution)/shard_map/jit(_take)/gather | solution.py:57
  305.6 10.3 %copy.33 = bf16[64,128,4,128]{3,1,0,2:T(8,128)(2,1)} copy(bf16[64,128,4,128]{3,1,2,0:T(8,128)(2,1)} %gather_fusion.2) | data formatting | bytes 16777216 | tf_op jit(solution)/shard_map/jit(_take)/gather | solution.py:57
  315.9 7.4 %bitcast_select_fusion = bf16[2,4096,4,128]{3,1,0,2:T(8,128)(2,1)} fusion(pred[2,4096]{1,0:T(4,128)(4,1)S(1)} %bitcast.85, bf16[2,4096,4,128]{3,1,0,2:T(8,128)(2,1)} %bitcast.83), kind=kLoop, calls=%fused_computation.24 | loop fusion | flops 4194304 | bytes 16785408 | tf_op jit(solution)/shard_map/jit(_take)/select_n | solution.py:57
  323.3 11.3 %copy.35 = bf16[2,4096,4,128]{1,3,2,0:T(8,128)(2,1)} copy(bf16[2,4096,4,128]{3,1,0,2:T(8,128)(2,1)} %bitcast_select_fusion) | data formatting | bytes 16777216 | tf_op jit(solution)/shard_map/while | solution.py:93
  334.6 120.4 %while.22 = (s32[]{:T(128)}, f32[4,256,4,64]{1,3,2,0:T(8,128)S(1)}, f32[4,2,4096]{2,1,0:T(2,128)}, bf16[4,256,4,64]{1,3,2,0:T(8,128)(2,1)}, bf16[2,4096,4,128]{1...) while((s32[]{:T(128)}, f32[4,256,4,64]{1,3,2,0:T(8,128)S(1)}, ...), condition=%wide.region_7.8_spmd, body=%wide.region_4.7_spmd.sunk | while | flops 1103233024 | bytes 14139656 | solution.py:93
  334.6 1.5 dynamic-slice_bitcast_fusion.6
  337.0 27.7 %while.23 = (s32[]{:T(128)}, f32[256,4,64]{0,2,1:T(8,128)S(1)}, bf16[2,4096,4,128]{1,3,2,0:T(8,128)(2,1)}, bf16[256,4,64]{0,2,1:T(8,128)(2,1)}, f32[2,4096]{1,0:T(2,128)S(1)}, /*index=5*/s32[]{:T(128)}, s32[]{:T(128)}) while((s32[]{:T(128)}, f32[256,4,64]{0,2,1:T(8,128)S(1)}, bf16[2,4096,4,128]{1,3,2,0:T(8,128)(2,1)}, ...), condition=%wide.region_6.6_spmd.clone, body=%wide.region_5.5_spmd.clone.sunk | while | flops 1103233024 | bytes 13287519 | solution.py:88
  337.0 4.7 dynamic-slice_bitcast_fusion.8
  341.6 9.2 %fusion.60 = f32[256,4,64]{0,2,1:T(8,128)S(1)} fusion(bf16[256,4,64]{0,2,1:T(8,128)(2,1)} %get-tuple-element.222, f32[4096]{0:T(1024)S(1)} %bitcast.84, bf16[4096,4,128]{0,2,1:T(8,128)(2,1)} %dynamic-slice_bitcast_fusion.8, f32[256,4,64]{0,2,1:T(8,128)S(1)} %get-tuple-element.213, pred[]{:T(512)S(6)} %compare.6), kind=kOutput, calls=%fused_computation.15.clone.1 | convolution fusion | flops 1103233024 | bytes 4866049 | tf_op jit(solution)/shard_map/while/body/eval_jaxpr/while/body/eval_jaxpr/hck,khd->chd/dot_general | solution.py:82
  350.8 4.7 dynamic-slice_bitcast_fusion.8
  355.5 9.2 %fusion.60 = f32[256,4,64]{0,2,1:T(8,128)S(1)} fusion(bf16[256,4,64]{0,2,1:T(8,128)(2,1)} %get-tuple-element.222, f32[4096]{0:T(1024)S(1)} %bitcast.84, bf16[4096,4,128]{0,2,1:T(8,128)(2,1)} %dynamic-slice_bitcast_fusion.8, f32[256,4,64]{0,2,1:T(8,128)S(1)} %get-tuple-element.213, pred[]{:T(512)S(6)} %compare.6), kind=kOutput, calls=%fused_computation.15.clone.1 | convolution fusion | flops 1103233024 | bytes 4866049 | tf_op jit(solution)/shard_map/while/body/eval_jaxpr/while/body/eval_jaxpr/hck,khd->chd/dot_general | solution.py:82
  364.7 1.5 dynamic-slice_bitcast_fusion.6
  367.1 27.7 %while.23 = (s32[]{:T(128)}, f32[256,4,64]{0,2,1:T(8,128)S(1)}, bf16[2,4096,4,128]{1,3,2,0:T(8,128)(2,1)}, bf16[256,4,64]{0,2,1:T(8,128)(2,1)}, f32[2,4096]{1,0:T(2,128)S(1)}, /*index=5*/s32[]{:T(128)}, s32[]{:T(128)}) while((s32[]{:T(128)}, f32[256,4,64]{0,2,1:T(8,128)S(1)}, bf16[2,4096,4,128]{1,3,2,0:T(8,128)(2,1)}, ...), condition=%wide.region_6.6_spmd.clone, body=%wide.region_5.5_spmd.clone.sunk | while | flops 1103233024 | bytes 13287519 | solution.py:88
  367.1 4.7 dynamic-slice_bitcast_fusion.8
  371.7 9.2 %fusion.60 = f32[256,4,64]{0,2,1:T(8,128)S(1)} fusion(bf16[256,4,64]{0,2,1:T(8,128)(2,1)} %get-tuple-element.222, f32[4096]{0:T(1024)S(1)} %bitcast.84, bf16[4096,4,128]{0,2,1:T(8,128)(2,1)} %dynamic-slice_bitcast_fusion.8, f32[256,4,64]{0,2,1:T(8,128)S(1)} %get-tuple-element.213, pred[]{:T(512)S(6)} %compare.6), kind=kOutput, calls=%fused_computation.15.clone.1 | convolution fusion | flops 1103233024 | bytes 4866049 | tf_op jit(solution)/shard_map/while/body/eval_jaxpr/while/body/eval_jaxpr/hck,khd->chd/dot_general | solution.py:82
  380.9 4.7 dynamic-slice_bitcast_fusion.8
  385.6 9.2 %fusion.60 = f32[256,4,64]{0,2,1:T(8,128)S(1)} fusion(bf16[256,4,64]{0,2,1:T(8,128)(2,1)} %get-tuple-element.222, f32[4096]{0:T(1024)S(1)} %bitcast.84, bf16[4096,4,128]{0,2,1:T(8,128)(2,1)} %dynamic-slice_bitcast_fusion.8, f32[256,4,64]{0,2,1:T(8,128)S(1)} %get-tuple-element.213, pred[]{:T(512)S(6)} %compare.6), kind=kOutput, calls=%fused_computation.15.clone.1 | convolution fusion | flops 1103233024 | bytes 4866049 | tf_op jit(solution)/shard_map/while/body/eval_jaxpr/while/body/eval_jaxpr/hck,khd->chd/dot_general | solution.py:82
  394.8 1.5 dynamic-slice_bitcast_fusion.6
  397.2 27.7 %while.23 = (s32[]{:T(128)}, f32[256,4,64]{0,2,1:T(8,128)S(1)}, bf16[2,4096,4,128]{1,3,2,0:T(8,128)(2,1)}, bf16[256,4,64]{0,2,1:T(8,128)(2,1)}, f32[2,4096]{1,0:T(2,128)S(1)}, /*index=5*/s32[]{:T(128)}, s32[]{:T(128)}) while((s32[]{:T(128)}, f32[256,4,64]{0,2,1:T(8,128)S(1)}, bf16[2,4096,4,128]{1,3,2,0:T(8,128)(2,1)}, ...), condition=%wide.region_6.6_spmd.clone, body=%wide.region_5.5_spmd.clone.sunk | while | flops 1103233024 | bytes 13287519 | solution.py:88
  397.2 4.7 dynamic-slice_bitcast_fusion.8
  401.8 9.2 %fusion.60 = f32[256,4,64]{0,2,1:T(8,128)S(1)} fusion(bf16[256,4,64]{0,2,1:T(8,128)(2,1)} %get-tuple-element.222, f32[4096]{0:T(1024)S(1)} %bitcast.84, bf16[4096,4,128]{0,2,1:T(8,128)(2,1)} %dynamic-slice_bitcast_fusion.8, f32[256,4,64]{0,2,1:T(8,128)S(1)} %get-tuple-element.213, pred[]{:T(512)S(6)} %compare.6), kind=kOutput, calls=%fused_computation.15.clone.1 | convolution fusion | flops 1103233024 | bytes 4866049 | tf_op jit(solution)/shard_map/while/body/eval_jaxpr/while/body/eval_jaxpr/hck,khd->chd/dot_general | solution.py:82
  411.0 4.7 dynamic-slice_bitcast_fusion.8
  415.7 9.2 %fusion.60 = f32[256,4,64]{0,2,1:T(8,128)S(1)} fusion(bf16[256,4,64]{0,2,1:T(8,128)(2,1)} %get-tuple-element.222, f32[4096]{0:T(1024)S(1)} %bitcast.84, bf16[4096,4,128]{0,2,1:T(8,128)(2,1)} %dynamic-slice_bitcast_fusion.8, f32[256,4,64]{0,2,1:T(8,128)S(1)} %get-tuple-element.213, pred[]{:T(512)S(6)} %compare.6), kind=kOutput, calls=%fused_computation.15.clone.1 | convolution fusion | flops 1103233024 | bytes 4866049 | tf_op jit(solution)/shard_map/while/body/eval_jaxpr/while/body/eval_jaxpr/hck,khd->chd/dot_general | solution.py:82
  425.0 1.5 dynamic-slice_bitcast_fusion.6
  427.3 27.7 %while.23 = (s32[]{:T(128)}, f32[256,4,64]{0,2,1:T(8,128)S(1)}, bf16[2,4096,4,128]{1,3,2,0:T(8,128)(2,1)}, bf16[256,4,64]{0,2,1:T(8,128)(2,1)}, f32[2,4096]{1,0:T(2,128)S(1)}, /*index=5*/s32[]{:T(128)}, s32[]{:T(128)}) while((s32[]{:T(128)}, f32[256,4,64]{0,2,1:T(8,128)S(1)}, bf16[2,4096,4,128]{1,3,2,0:T(8,128)(2,1)}, ...), condition=%wide.region_6.6_spmd.clone, body=%wide.region_5.5_spmd.clone.sunk | while | flops 1103233024 | bytes 13287519 | solution.py:88
  427.3 4.7 dynamic-slice_bitcast_fusion.8
  431.9 9.2 %fusion.60 = f32[256,4,64]{0,2,1:T(8,128)S(1)} fusion(bf16[256,4,64]{0,2,1:T(8,128)(2,1)} %get-tuple-element.222, f32[4096]{0:T(1024)S(1)} %bitcast.84, bf16[4096,4,128]{0,2,1:T(8,128)(2,1)} %dynamic-slice_bitcast_fusion.8, f32[256,4,64]{0,2,1:T(8,128)S(1)} %get-tuple-element.213, pred[]{:T(512)S(6)} %compare.6), kind=kOutput, calls=%fused_computation.15.clone.1 | convolution fusion | flops 1103233024 | bytes 4866049 | tf_op jit(solution)/shard_map/while/body/eval_jaxpr/while/body/eval_jaxpr/hck,khd->chd/dot_general | solution.py:82
  441.1 4.7 dynamic-slice_bitcast_fusion.8
  445.8 9.2 %fusion.60 = f32[256,4,64]{0,2,1:T(8,128)S(1)} fusion(bf16[256,4,64]{0,2,1:T(8,128)(2,1)} %get-tuple-element.222, f32[4096]{0:T(1024)S(1)} %bitcast.84, bf16[4096,4,128]{0,2,1:T(8,128)(2,1)} %dynamic-slice_bitcast_fusion.8, f32[256,4,64]{0,2,1:T(8,128)S(1)} %get-tuple-element.213, pred[]{:T(512)S(6)} %compare.6), kind=kOutput, calls=%fused_computation.15.clone.1 | convolution fusion | flops 1103233024 | bytes 4866049 | tf_op jit(solution)/shard_map/while/body/eval_jaxpr/while/body/eval_jaxpr/hck,khd->chd/dot_general | solution.py:82
  455.2 1.8 copy.41
  457.0 2.5 reshape.211
  459.5 11.9 %all-reduce = (f32[1024]{0:T(1024)S(1)}, f32[1024]{0:T(1024)S(1)}) all-reduce(f32[1024]{0:T(1024)S(1)} %bitcast.91, f32[1024]{0:T(1024)S(1)} %bitcast.90), channel_id=1, replica_groups=mesh['cache'=32,'item'=4] {'item'}, use_global_device_ids=true, to_apply=%region_11.12 | all-reduce | flops 2048 | bytes 16384 | tf_op jit(solution)/shard_map/psum | solution.py:98
  471.4 5.8 %fusion.22 = f32[1024,1024]{1,0:T(8,128)} fusion(f32[1024,256]{1,0:T(8,128)S(1)} %reshape.211, bf16[1024,1024]{1,0:T(8,128)(2,1)S(1)} %copy-done, s32[]{:T(128)S(6)} %select_n.105, bf16[1024,1024]{1,0:T(8,128)(2,1)} %all-reduce.3.cloned.1.call-done, bf16[1024,1024]{1,0:T(8,128)(2,1)} %param.19, f32[256]{0:T(256)S(1)} %copy-done.3, ...), kind=kOutput, calls=%fused_computation.31 | convolution fusion | flops 1076101120 | bytes 8398848 | tf_op jit(solution)/shard_map/dot_general | solution.py:106
  477.3 73.7 %reduce-scatter.2.cloned.1.call-done = f32[256,1024]{1,0:T(8,128)} async-done(((f32[1024,1024]{1,0:T(8,128)}), f32[256,1024]{1,0:T(8,128)}) %reduce-scatter.2.cloned.1.call-update) | async-done | bytes 1048592 | tf_op jit(solution)/shard_map/reduce_scatter | solution.py:105
  551.0 2.3 fusion.23
  (63 shorter events, 7.5 us)
Async XLA Ops:
  6.5 464.9 %copy-start = (bf16[1024,1024]{1,0:T(8,128)(2,1)S(1)}, bf16[1024,1024]{1,0:T(8,128)(2,1)}, u32[]{:S(2)}) copy-start(bf16[1024,1024]{1,0:T(8,128)(2,1)} %param.21) | copy-start | bytes 6291460
  45.0 8.4 %copy-start.1 = (s32[1,1024]{1,0:T(1,128)S(1)}, s32[1,1024]{1,0:T(1,128)}, u32[]{:S(2)}) copy-start(s32[1,1024]{1,0:T(1,128)} %param.13) | copy-start | bytes 12292
  45.0 249.3 %all-to-all-start = ((bf16[32,4,128,4,128]{4,2,3,1,0:T(8,128)(2,1)}), bf16[32,4,128,4,128]{4,2,3,1,0:T(8,128)(2,1)}, u32[]{:S(2)}, u32[]{:S(2)}) async-start(bf16[32,4,128,4,128]{4,2,3,1,0:T(8,128)(2,1)} %fusion.21), calls=%async_computation | async-start | bytes 33554432 | tf_op jit(solution)/shard_map/all_to_all | solution.py:53
  53.4 73.5 %all-reduce.3.cloned.1.call-start = ((), (), s32[]{:S(2)}) async-start(), calls=%async_computation.2 | async-start | bytes 4194304 | tf_op jit(solution)/shard_map/psum | solution.py:29
  62.2 4.8 copy-start.2
  65.4 485.5 %reduce-scatter.2.cloned.1.call-start = ((), (), s32[]{:S(2)}) async-start(), calls=%async_computation.3 | async-start | bytes 5242880 | tf_op jit(solution)/shard_map/reduce_scatter | solution.py:105
  455.1 16.4 %copy-start.3 = (f32[256]{0:T(256)S(1)}, f32[256]{0:T(256)}, u32[]{:S(2)}) copy-start(f32[256]{0:T(256)} %dynamic_slice.38) | copy-start | bytes 3076
Sparse Core Ops, SparseCore 0:
  65.5 61.3 all-reduce.2
  477.4 73.4 reduce-scatter.1
where the time goes:
time: 562 us; the launch traced here: 560 us
  waiting for transfers between devices  291 us (52%)
  local copies, waits for them, and re-layouts  121 us (22%)
  matrix products  82.4 us (15%)
  other arithmetic  31.9 us (6%)
  between operations  13.6 us (2%)
  blocking collectives  11.9 us (2%)
  starting transfers between devices  8.62 us (2%)
    all_to_all x1, waiting for transfers between devices, on_device(): lax.all_to_all(outgoing, 'cache', split_axis=0, concat_axis=0, tiled=True)  159 us
    reduce_scatter x1, waiting for transfers between devices, on_device(): lax.psum_scatter(jnp.dot(hidden, out_part, preferred_element_type=jnp.flo...  73.7 us
    dot_general x8, matrix products, over_group(): jnp.einsum('hck,khd->chd', weights, kv_group[:, :, DH:], preferred_elemen...  73.3 us
    psum x1, waiting for transfers between devices, on_device(): lax.psum(term_rows, 'item').astype(jnp.float32).astype(jnp.bfloat16)  57.7 us
    squeeze x8, local copies, waits for them, and re-layouts, one_block(): lax.scan(over_group, jnp.zeros((CB, heads_here, DH), jnp.float32), (group...  37.3 us
    gather x2, local copies, waits for them, and re-layouts, on_device(): history = jnp.take(received, my_owner * SLOT + my_rank, axis=0)  21.6 us
    gather x1, local copies, waits for them, and re-layouts, on_device(): outgoing = jnp.take(kv_cache, local_block.reshape(-1), axis=0)  19.9 us
    select_n x1, other arithmetic, on_device(): jnp.where(filled.reshape(-1)[:, None, None, None], outgoing, jnp.zeros(()...  15.3 us
  transfers between devices with their start and end apart: 3, of which 3 were waited for; matrix products, arithmetic and copies ran while one was open for 4% of the time, Pallas kernels for 0%

commit v1 on v0

v1 whole, which is shorter than its diff:
```python
import functools
import jax
import jax.numpy as jnp
from jax import lax
from jax.experimental import pallas as pl
from jax.experimental.pallas import tpu as pltpu
from jax.sharding import PartitionSpec as P

DH = 64
BLK = 128
SLOT = 4
CB = 256
RING = 4
SOURCES = 8
GROUP = 4
PHASES = ((2, 1), (3, 0))

norm_eps = 1e-05


def at(x, y, core):
    return ((x % RING) * RING + y % RING) * 2 + core


def kv_pairs(j, s):
    pairs = []
    for x in range(RING):
        for y in range(RING):
            for core in range(2):
                dest = at(x, y + j, 0) if core == s else at(x + j, y, 1)
                pairs.append((at(x, y, core), dest))
    return pairs


def ring_pairs(k):
    pairs = []
    for x in range(RING):
        for y in range(RING):
            pairs.append((at(x, y, 0), at(x + k, y, 0)))
            pairs.append((at(x, y, 1), at(x, y + k, 1)))
    return pairs


def pack_kernel(phases, here_ref, send_ref, kv_ref, *rest):
    outs, sems = rest[:-1], rest[-1]
    x, y, core = here_ref[0], here_ref[1], here_ref[2]

    def copies(run):
        for p, ks in enumerate(phases):
            for i in range(SOURCES):
                j, s = i // 2, i % 2
                same = core == s
                for kk, k in enumerate(ks):
                    rx = lax.rem(jnp.where(same, x + k, x + j), RING)
                    ry = lax.rem(jnp.where(same, y + j, y + k), RING)
                    request = (rx * RING + ry) * 2 + jnp.where(same, 0, 1)

                    def slot_step(slot, carry, p=p, i=i, kk=kk, k=k, request=request):
                        block = send_ref[request * SLOT + slot]

                        @pl.when(block >= 0)
                        def _():
                            run(
                                pltpu.make_async_copy(
                                    kv_ref.at[jnp.maximum(block, 0)],
                                    outs[p * SOURCES + i].at[kk, slot],
                                    sems.at[(i * RING + k) * SLOT + slot],
                                )
                            )

                        return carry

                    lax.fori_loop(0, SLOT, slot_step, 0)

    copies(lambda c: c.start())
    copies(lambda c: c.wait())


def pack(here, send, kv, phases):
    outs = []
    for ks in phases:
        outs += [jax.ShapeDtypeStruct((len(ks), SLOT) + kv.shape[1:], kv.dtype)] * SOURCES
    smem = pl.BlockSpec(memory_space=pltpu.SMEM)
    hbm = pl.BlockSpec(memory_space=pl.ANY)
    return pl.pallas_call(
        functools.partial(pack_kernel, phases),
        out_shape=outs,
        in_specs=[smem, smem, pl.BlockSpec(memory_space=pltpu.VMEM)],
        out_specs=[hbm] * len(outs),
        scratch_shapes=[pltpu.SemaphoreType.DMA((SOURCES * RING * SLOT,))],
        compiler_params=pltpu.CompilerParams(vmem_limit_bytes=40 * 2**20),
        cost_estimate=pl.CostEstimate(flops=0, bytes_accessed=16 * 2**20, transcendentals=0),
        name="pack",
    )(here, send, kv)


def attend_kernel(nk, cblks, heads, count_ref, list_ref, *rest):
    q_refs, kv_refs = rest[:nk], rest[nk : nk + SOURCES]
    o_refs = rest[nk + SOURCES : 2 * nk + SOURCES]
    held, queries, acc, sems = rest[2 * nk + SOURCES :]
    entries = SOURCES * SLOT
    stride = entries + GROUP

    def copy(k, i):
        return pltpu.make_async_copy(
            kv_refs[i].at[k], held.at[k, pl.ds(i * SLOT, SLOT)], sems.at[k * SOURCES + i]
        )

    for k in range(nk):
        for i in range(SOURCES):
            copy(k, i).start()
        held[k, entries] = jnp.zeros(held.shape[2:], held.dtype)
    for k in range(nk):
        for h in range(heads):
            queries[h] = q_refs[k][:, h * DH : (h + 1) * DH]
        for i in range(SOURCES):
            copy(k, i).wait()

        def one_cblk(c, carry, k=k):
            rows = pl.ds(pl.multiple_of(c * CB, CB), CB)
            acc[...] = jnp.zeros_like(acc)

            def group(g, carry):
                base = (k * cblks + c) * stride + g * GROUP
                ids = [list_ref[base + i] for i in range(GROUP)]
                kvs = [
                    jnp.concatenate([held[k, e, h] for e in ids], axis=0) for h in range(heads)
                ]
                halves = [
                    lax.dot_general(
                        queries[h, rows, :],
                        kvs[h][:, :DH],
                        (((1,), (1,)), ((), ())),
                        preferred_element_type=jnp.float32,
                    )
                    for h in range(heads)
                ]
                weights = [(s + s * jnp.tanh(s)).astype(jnp.bfloat16) for s in halves]
                for h in range(heads):
                    acc[h] += jnp.dot(weights[h], kvs[h], preferred_element_type=jnp.float32)
                return carry

            groups = (count_ref[k * cblks + c] + GROUP - 1) // GROUP
            lax.fori_loop(0, groups, group, 0)
            o_refs[k][rows, :] = jnp.concatenate(
                [acc[h][:, DH:] for h in range(heads)], axis=1
            ).astype(o_refs[k].dtype)
            return carry

        lax.fori_loop(0, cblks, one_cblk, 0)


def attend(counts, lists, qs, kvs):
    nk = len(qs)
    rows, width = qs[0].shape
    heads = width // DH
    cblks = rows // CB
    smem = pl.BlockSpec(memory_space=pltpu.SMEM)
    vmem = pl.BlockSpec(memory_space=pltpu.VMEM)
    hbm = pl.BlockSpec(memory_space=pl.ANY)
    entries = SOURCES * SLOT
    work = nk * cblks * heads * CB * BLK * entries
    return pl.pallas_call(
        functools.partial(attend_kernel, nk, cblks, heads),
        out_shape=[jax.ShapeDtypeStruct((rows, width), jnp.bfloat16)] * nk,
        in_specs=[smem, smem] + [vmem] * nk + [hbm] * SOURCES,
        out_specs=[vmem] * nk,
        scratch_shapes=[
            pltpu.VMEM((nk, entries + 1, heads, BLK, 2 * DH), jnp.bfloat16),
            pltpu.VMEM((heads, rows, DH), jnp.bfloat16),
            pltpu.VMEM((heads, CB, 2 * DH), jnp.float32),
            pltpu.SemaphoreType.DMA((nk * SOURCES,)),
        ],
        compiler_params=pltpu.CompilerParams(vmem_limit_bytes=40 * 2**20),
        cost_estimate=pl.CostEstimate(
            flops=16 * work * DH, bytes_accessed=nk * 6 * 2**20, transcendentals=work
        ),
        name="attend",
    )(counts, lists, *qs, *kvs)


def on_device(
    cand_items, item_table, kv_cache, hist_blocks, pattern, w_query, w_gate, norm_gain, w_out
):
    zs = lax.axis_size("item")
    z = lax.axis_index("item")
    me = lax.axis_index("cache")
    core, y, x = me % 2, (me // 2) % RING, me // (2 * RING)
    on0 = core == 0
    blocks_here = kv_cache.shape[0]
    list_len = hist_blocks.shape[1]
    width = w_gate.shape[0]
    ring = lambda d: [(i, (i + d) % zs) for i in range(zs)]

    owner_of = hist_blocks // blocks_here
    local_of = hist_blocks % blocks_here
    same_owner = owner_of[:, :, None] == owner_of[:, None, :]
    positions = jnp.arange(list_len)
    earlier = positions[None, :] < positions[:, None]
    slot_rank = jnp.sum(same_owner & earlier[None], axis=2)
    slots = jnp.arange(SLOT)
    selected = (owner_of == me)[:, None, :] & (slot_rank[:, None, :] == slots[None, :, None])
    send = jnp.sum(jnp.where(selected, local_of[:, None, :] + 1, 0), axis=2) - 1
    here = jnp.stack([x, y, core]).astype(jnp.int32)
    kv_heads = kv_cache.transpose(0, 2, 1, 3)
    packed = pack(here, send.reshape(-1).astype(jnp.int32), kv_heads, PHASES)
    arrived = []
    for p in range(len(PHASES)):
        for i in range(SOURCES):
            block = packed[p * SOURCES + i]
            arrived.append(block if i == 0 else lax.ppermute(block, "cache", kv_pairs(i // 2, i % 2)))

    item_ids = cand_items[0]
    table_rows = item_table.shape[0]
    rows_per = item_ids.shape[0] // zs

    def picked(d):
        ids = lax.dynamic_slice_in_dim(item_ids, ((z + d) % zs) * rows_per, rows_per, 0)
        local = ids - z * table_rows
        inside = (local >= 0) & (local < table_rows)
        taken = jnp.take(item_table, jnp.clip(local, 0, table_rows - 1), axis=0)
        return jnp.where(inside[:, None], taken, jnp.zeros((), taken.dtype))

    embedded = picked(0)
    for d in range(1, zs):
        embedded = embedded + lax.ppermute(picked(d), "item", ring(d))
    chunks = [embedded] + [lax.ppermute(embedded, "item", ring(d)) for d in range(1, zs)]
    queries = jax.nn.silu(
        jnp.dot(jnp.concatenate(chunks, axis=0), w_query, preferred_element_type=jnp.float32)
    ).astype(jnp.bfloat16)
    queries = queries * jnp.asarray(0.5 * DH ** (-0.5), jnp.bfloat16)
    q_of = {0: queries}
    for k in range(1, RING):
        q_of[k] = lax.ppermute(queries, "cache", ring_pairs(-k))

    pattern_all = lax.all_gather(pattern[0], "cache")
    sources = jnp.arange(SOURCES)
    src_j, src_s = sources // 2, sources % 2
    owner_idx = jnp.where(
        on0, at(x, y - src_j + RING, src_s), at(x - src_j + RING, y, 1 - src_s)
    )
    order = [k for ks in PHASES for k in ks]
    k_arr = jnp.array(order)
    request = jnp.where(on0, at(x + k_arr, y, 0), at(x, y + k_arr, 1))
    owner_k = owner_of[request]
    rank_k = slot_rank[request]
    rotation = (z - jnp.arange(zs)) % zs
    pattern_k = pattern_all[request][:, rotation]
    entry_of = jnp.sum(
        jnp.where(owner_k[:, None, :] == owner_idx[None, :, None], sources[None, :, None] + 1, 0), axis=1
    ) - 1
    entry_of = jnp.where(entry_of >= 0, entry_of * SLOT + rank_k, -1)
    wanted = (pattern_k != 0) & (entry_of >= 0)[:, None, :]
    before = jnp.sum(
        (wanted[:, :, None, :] & earlier[None, None]).astype(jnp.int32), axis=3
    )
    entries = SOURCES * SLOT
    places = jnp.arange(entries + GROUP)
    lists = entries + jnp.sum(
        jnp.where(
            wanted[:, :, None, :] & (before[:, :, None, :] == places[None, None, :, None]),
            entry_of[:, None, None, :] - entries,
            0,
        ),
        axis=3,
    )
    counts = jnp.sum(wanted.astype(jnp.int32), axis=2)

    partial = {}
    base = 0
    for p, ks in enumerate(PHASES):
        outs = attend(
            counts[base : base + len(ks)].reshape(-1).astype(jnp.int32),
            lists[base : base + len(ks)].reshape(-1).astype(jnp.int32),
            [q_of[k] for k in ks],
            arrived[p * SOURCES : (p + 1) * SOURCES],
        )
        base += len(ks)
        for k, o in zip(ks, outs):
            partial[k] = o
    attended = partial[0].astype(jnp.float32)
    for k in range(1, RING):
        attended = attended + lax.ppermute(partial[k], "cache", ring_pairs(k)).astype(jnp.float32)

    pieces = []
    for i in range(zs):
        piece = attended[i * rows_per : (i + 1) * rows_per]
        pieces.append(piece if i == 0 else lax.ppermute(piece, "item", ring(-i)))
    doubled = jnp.concatenate(pieces + pieces[:-1], axis=1)
    attended = lax.dynamic_slice_in_dim(doubled, ((zs - z) % zs) * pieces[0].shape[1], width, 1)

    gate_act = jax.nn.silu(jnp.dot(embedded, w_gate, preferred_element_type=jnp.float32))
    row_mean = jnp.mean(attended, axis=1, keepdims=True)
    row_var = jnp.mean(attended * attended, axis=1, keepdims=True) - row_mean * row_mean
    normed = (attended - row_mean) * lax.rsqrt(row_var + norm_eps)
    hidden = (normed * norm_gain[None, :] * gate_act).astype(jnp.bfloat16)
    projected = jnp.dot(hidden, w_out, preferred_element_type=jnp.float32)
    return (embedded.astype(jnp.float32) + projected).astype(jnp.bfloat16)[None]


def solution(mesh):
    placed = (
        P("cache", None),
        P("item", None),
        P("cache", None, "item", None),
        P(),
        P("cache", None, None),
        P(None, "item"),
        P(),
        P(),
        P(),
    )
    return jax.shard_map(
        on_device, mesh=mesh, in_specs=placed, out_specs=P("cache", "item", None), check_vma=False
    )
```

time: 562 us -> 313 us (0.56)
  waiting for transfers between devices: 291 us -> 97.6 us
  matrix products: 82.4 us -> 5.9 us
  Pallas kernels: 0 us -> 59.8 us
  local copies, waits for them, and re-layouts: 121 us -> 62.1 us
  starting transfers between devices: 8.62 us -> 44.5 us
  other arithmetic: 31.9 us -> 15.4 us
  blocking collectives: 11.9 us -> 25.6 us
  between operations: 13.6 us -> 0.39 us
    all_to_all x1 -> x0, waiting for transfers between devices: 159 us -> none  [on_device(): lax.all_to_all(outgoing, 'cache', split_axis=0, concat_axis=0, tiled=True)]
    ppermute x0 -> x29, waiting for transfers between devices: none -> 97.6 us  [the longest x14 61.4 us: on_device(): lax.ppermute(block, 'cache', kv_pairs(i // 2, i % 2))]
    dot_general x10 -> x2, matrix products: 82.4 us -> 5.9 us  [the longest x1 4.35 us: on_device(): projected = jnp.dot(hidden, w_out, preferred_element_type=jnp.float32)]
    reduce_scatter x1 -> x0, waiting for transfers between devices: 73.7 us -> none  [on_device(): lax.psum_scatter(jnp.dot(hidden, out_part, preferred_element_type=jnp.flo...]
    pallas_call x0 -> x3, Pallas kernels: none -> 59.8 us  [the longest x2 49 us: attend(): pl.pallas_call(functools.partial(attend_kernel, nk, cblks, heads), out_sh...]
    psum x1 -> x0, waiting for transfers between devices: 57.7 us -> none  [on_device(): lax.psum(term_rows, 'item').astype(jnp.float32).astype(jnp.bfloat16)]
    squeeze x16 -> x0, local copies, waits for them, and re-layouts: 46.5 us -> none  [the longest x8 37.3 us: one_block(): lax.scan(over_group, jnp.zeros((CB, heads_here, DH), jnp.float32), (group...]
    ppermute x0 -> x29, starting transfers between devices: none -> 44.5 us  [the longest x14 20.9 us: on_device(): lax.ppermute(block, 'cache', kv_pairs(i // 2, i % 2))]
  transfers between devices with their start and end apart: 3 -> 29, of which waited for: 3 -> 8; matrix products, arithmetic and copies ran while one was open for 4% -> 12% of each run, Pallas kernels for 0% -> 16%
where the time goes in v1:
time: 313 us; the launch traced here: 311 us
  waiting for transfers between devices  97.6 us (31%)
  local copies, waits for them, and re-layouts  62.1 us (20%)
  Pallas kernels  59.8 us (19%)
  starting transfers between devices  44.5 us (14%)
  blocking collectives  25.6 us (8%)
  other arithmetic  15.4 us (5%)
  matrix products  5.9 us (2%)
    ppermute x14, waiting for transfers between devices, on_device(): lax.ppermute(block, 'cache', kv_pairs(i // 2, i % 2))  61.4 us
    pallas_call x2, Pallas kernels, attend(): pl.pallas_call(functools.partial(attend_kernel, nk, cblks, heads), out_sh...  49 us
    unnamed x64, local copies, waits for them, and re-layouts  35.8 us
    all_gather x1, blocking collectives, on_device(): pattern_all = lax.all_gather(pattern[0], 'cache')  25.6 us
    ppermute x14, starting transfers between devices, on_device(): lax.ppermute(block, 'cache', kv_pairs(i // 2, i % 2))  20.9 us
    gather x4, local copies, waits for them, and re-layouts, picked(): taken = jnp.take(item_table, jnp.clip(local, 0, table_rows - 1), axis=0)  20.3 us
    ppermute x3, waiting for transfers between devices, on_device(): lax.ppermute(embedded, 'item', ring(d))  18.3 us
    pallas_call x1, Pallas kernels, pack(): pl.pallas_call(functools.partial(pack_kernel, phases), out_shape=outs, in...  10.8 us
  transfers between devices with their start and end apart: 29, of which 8 were waited for; matrix products, arithmetic and copies ran while one was open for 12% of the time, Pallas kernels for 16%

profile of v1, /device:TPU:0, one launch (start us, length us, event | category | flops | bytes accessed | tf_op | source)
XLA Modules:
  0.0 311.2 jit_solution(4856302745178668934)
XLA Ops:
  2.9 9.1 %copy.42 = bf16[64,128,4,128]{3,1,2,0:T(8,128)(2,1)} copy(bf16[64,128,4,128]{3,2,1,0:T(4,128)(2,1)} %param.14) | data formatting | bytes 16777216 | tf_op args[2]
  12.1 10.8 %pack.1 = (bf16[2,4,4,128,128]{4,3,2,1,0:T(8,128)(2,1)S(1)}, bf16[2,4,4,128,128]{4,3,2,1,0:T(8,128)(2,1)}, bf16[2,4,4,128,128]{4,3,2,1,0:T(8,128)(2,1)}, bf16[2,...) custom-call(s32[3]{0:T(128)S(1)} %pad_add_fusion.here_ref, ...), custom_call_target="tpu_custom_call" | custom-call | bytes 16777216 | tf_op jit(solution)/shard_map/pack/pallas_call | solution.py:85
  24.9 1.0 copy-done.3
  29.8 1.1 copy-done.11
  31.8 10.1 %collective-permute-start.16 = (bf16[2,4,4,128,128]{4,3,2,1,0:T(8,128)(2,1)}, bf16[2,4,4,128,128]{4,3,2,1,0:T(8,128)(2,1)}, u32[]{:S(2)}, u32[]{:S(2)}) collective-permute-start(bf16[2,4,4,128,128]{4,3,2,1,0:T(8,128)(2,1)} %get-tuple-element.36), channel_id=1, source_target_pairs={{0,4},{4,0},{8,12},{12,8},{16,20},{20,16},{24,28},{28,24},{32,36},... | collective-permute-start | bytes 3145736 | tf_op jit(solution)/shard_map/ppermute | solution.py:211
  42.0 5.1 %gather_fusion.6 = bf16[256,1024]{1,0:T(8,128)(2,1)} fusion(bf16[2048,1024]{1,0:T(8,128)(2,1)} %param.13, s32[1024]{0:T(1024)S(1)} %pad_clamp_fusion.3), kind=kCustom, calls=%fused_computation.2.clone | custom fusion | bytes 1049600 | tf_op jit(solution)/shard_map/jit(_take)/gather | solution.py:221
  47.1 2.0 select_select_fusion.1
  49.0 4.7 %collective-permute-start.1 = (bf16[256,1024]{1,0:T(8,128)(2,1)}, bf16[256,1024]{1,0:T(8,128)(2,1)}, u32[]{:S(2)}, u32[]{:S(2)}) collective-permute-start(bf16[256,1024]{1,0:T(8,128)(2,1)} %select_select_fusion.1), channel_id=1, source_target_pairs={{0,2},{1,3},{2,0},{3,1},{4,6},{5,7},{6,4},{7,5},{8,10},{9,11},{10,... | collective-permute-start | bytes 1572872 | tf_op jit(solution)/shard_map/ppermute | solution.py:226
  53.8 5.1 %gather_fusion.5 = bf16[256,1024]{1,0:T(8,128)(2,1)} fusion(bf16[2048,1024]{1,0:T(8,128)(2,1)} %param.13, s32[1024]{0:T(1024)S(1)} %pad_clamp_fusion.4), kind=kCustom, calls=%fused_computation.1.clone | custom fusion | bytes 1049600 | tf_op jit(solution)/shard_map/jit(_take)/gather | solution.py:221
  58.9 2.0 select_select_fusion.2
  60.8 1.0 collective-permute-start
  61.9 5.1 %gather_fusion.7 = bf16[256,1024]{1,0:T(8,128)(2,1)} fusion(bf16[2048,1024]{1,0:T(8,128)(2,1)} %param.13, s32[1024]{0:T(1024)S(1)} %pad_clamp_fusion.2), kind=kCustom, calls=%fused_computation.3.clone | custom fusion | bytes 1049600 | tf_op jit(solution)/shard_map/jit(_take)/gather | solution.py:221
  67.0 2.0 select_select_fusion
  68.9 2.2 collective-permute-start.2
  72.3 5.1 %gather_fusion.4 = bf16[256,1024]{1,0:T(8,128)(2,1)} fusion(bf16[2048,1024]{1,0:T(8,128)(2,1)} %param.13, s32[1024]{0:T(1024)S(1)} %pad_clamp_fusion.5), kind=kCustom, calls=%fused_computation.clone | custom fusion | bytes 1049600 | tf_op jit(solution)/shard_map/jit(_take)/gather | solution.py:221
  77.4 25.6 %all_gather.3 = s32[32,4,64]{2,1,0:T(4,128)S(1)} all-gather(s32[1,4,64]{2,1,0:T(4,128)S(1)} %copy-done.25), channel_id=1, replica_groups=mesh['cache'=32,'item'=4] {'cache'}, dimensions={0}, use_global_device_ids=true | all-gather | bytes 33792 | tf_op jit(solution)/shard_map/all_gather | solution.py:236
  104.7 2.1 collective-permute-start.19
  107.8 1.7 fusion.16
  109.6 2.9 collective-permute-start.21
  112.8 29.6 %collective-permute-done.18.rest_5_ = bf16[2,4,4,128,128]{4,3,2,1,0:T(8,128)(2,1)S(1)} collective-permute-done((bf16[2,4,4,128,128]{4,3,2,1,0:T(8,128)(2,1)}, bf16[2,4,4,128,128]{4,3,2,1,0:T(8,128)(2,1)S(1)}, u32[]{:S(2)}, u32[]{:S(2)}) %collective-permute-start.18) | collective-permute-done | bytes 1048608 | tf_op jit(solution)/shard_map/ppermute | solution.py:211
  144.4 1.5 collective-permute-start.4
  146.8 1.8 collective-permute-start.5
  149.1 2.5 select_reduce_fusion
  151.6 18.3 %collective-permute-done.3 = bf16[256,1024]{1,0:T(8,128)(2,1)S(1)} collective-permute-done((bf16[256,1024]{1,0:T(8,128)(2,1)S(1)}, bf16[256,1024]{1,0:T(8,128)(2,1)S(1)}, u32[]{:S(2)}, u32[]{:S(2)}) %collective-permute-start.3) | collective-permute-done | bytes 524320 | tf_op jit(solution)/shard_map/ppermute | solution.py:227
  170.0 2.4 collective-permute-start.11
  172.3 1.5 fusion.10.rest_1_
  176.9 20.8 %collective-permute-done.10.rest_6_ = bf16[2,4,4,128,128]{4,3,2,1,0:T(8,128)(2,1)} collective-permute-done((bf16[2,4,4,128,128]{4,3,2,1,0:T(8,128)(2,1)}, bf16[2,4,4,128,128]{4,3,2,1,0:T(8,128)(2,1)}, u32[]{:S(2)}, u32[]{:S(2)}) %collective-permute-start.10) | collective-permute-done | bytes 1048608 | tf_op jit(solution)/shard_map/ppermute | solution.py:211
  197.8 11.0 %collective-permute-done.12.rest_8_ = bf16[2,4,4,128,128]{4,3,2,1,0:T(8,128)(2,1)} collective-permute-done((bf16[2,4,4,128,128]{4,3,2,1,0:T(8,128)(2,1)}, bf16[2,4,4,128,128]{4,3,2,1,0:T(8,128)(2,1)}, u32[]{:S(2)}, u32[]{:S(2)}) %collective-permute-start.12) | collective-permute-done | bytes 1048608 | tf_op jit(solution)/shard_map/ppermute | solution.py:211
  208.8 1.8 collective-permute-start.9
  210.5 3.9 %collective-permute-start.6 = (bf16[1024,256]{1,0:T(8,128)(2,1)}, bf16[1024,256]{1,0:T(8,128)(2,1)S(1)}, u32[]{:S(2)}, u32[]{:S(2)}) collective-permute-start(bf16[1024,256]{1,0:T(8,128)(2,1)} %fusion.10.rest_1_), channel_id=1, source_target_pairs={{0,32},{4,12},{8,40},{12,20},{16,48},{20,28},{24,56},{28,4},{32,64... | collective-permute-start | bytes 1572872 | tf_op jit(solution)/shard_map/ppermute | solution.py:234
  214.5 1.2 copy-done.5
  215.7 1.2 copy-done.14
  216.9 1.2 copy-done.16
  218.1 1.2 copy-done.18
  219.4 1.2 copy-done.20
  220.6 1.2 copy-done.22
  221.8 24.1 %attend.3 = (bf16[1024,256]{1,0:T(8,128)(2,1)S(1)}, bf16[1024,256]{1,0:T(8,128)(2,1)S(1)}) custom-call(s32[8]{0:T(128)S(1)} %reshape.284.count_ref, s32[288]{0:T(512)S(1)} %reshape.285.list_ref, bf16[1024,256]{1,0:T(8,128)(2,1)} %collective-permute-done.14.rest_0_, bf16[1024,256]{1,0:T(8,128)(2,1)} %collective-permute-done.15.rest_1_, ...), custom_call_target="tpu_custom_call" | custom-call | flops 34359738368 | bytes 12582912 | tf_op jit(solution)/shard_map/attend/pallas_call | solution.py:163
  246.0 6.0 %collective-permute-start.24 = (bf16[1024,256]{1,0:T(8,128)(2,1)S(1)}, bf16[1024,256]{1,0:T(8,128)(2,1)S(1)}, u32[]{:S(2)}, u32[]{:S(2)}) collective-permute-start(bf16[1024,256]{1,0:T(8,128)(2,1)S(1)} %get-tuple-element.44), channel_id=1, source_target_pairs={{0,64},{4,20},{8,72},{12,28},{16,80},{20,4},{24,88},{28,12},{32,96... | collective-permute-start | bytes 1572872 | tf_op jit(solution)/shard_map/ppermute | solution.py:283
  252.0 24.9 %attend.2 = (bf16[1024,256]{1,0:T(8,128)(2,1)S(1)}, bf16[1024,256]{1,0:T(8,128)(2,1)S(1)}) custom-call(s32[8]{0:T(128)S(1)} %reshape.282.count_ref, s32[288]{0:T(512)S(1)} %reshape.283.list_ref, bf16[1024,256]{1,0:T(8,128)(2,1)S(1)} %collective-permute-done.6.rest_0_, bf16[1024,256]{1,0:T(8,128)(2,1)} %fusion.10.rest_1_, ...), custom_call_target="tpu_custom_call" | custom-call | flops 34359738368 | bytes 12582912 | tf_op jit(solution)/shard_map/attend/pallas_call | solution.py:163
  277.0 9.1 %collective-permute-done.25 = bf16[1024,256]{1,0:T(8,128)(2,1)S(1)} collective-permute-done((bf16[1024,256]{1,0:T(8,128)(2,1)S(1)}, bf16[1024,256]{1,0:T(8,128)(2,1)S(1)}, u32[]{:S(2)}, u32[]{:S(2)}) %collective-permute-start.25) | collective-permute-done | bytes 524320 | tf_op jit(solution)/shard_map/ppermute | solution.py:283
  287.4 2.0 collective-permute-start.28
  289.4 6.7 %collective-permute-done.26 = f32[256,256]{1,0:T(8,128)S(1)} collective-permute-done((f32[256,256]{1,0:T(8,128)}, f32[256,256]{1,0:T(8,128)S(1)}, u32[]{:S(2)}, u32[]{:S(2)}) %collective-permute-start.26) | collective-permute-done | bytes 262176 | tf_op jit(solution)/shard_map/ppermute | solution.py:288
  297.8 1.7 constant_dynamic-update-slice_fusion.3
  299.5 1.0 collective-permute-done.28
  300.5 1.7 constant_dynamic-update-slice_fusion.2
  303.7 1.7 constant_dynamic-update-slice_fusion
  305.4 1.4 dynamic-slice_reduce_fusion
  306.9 4.3 %fusion.13 = bf16[1,256,1024]{2,1,0:T(8,128)(2,1)} fusion(bf16[256,1024]{1,0:T(8,128)(2,1)} %copy-done.23, bf16[1024,1024]{1,0:T(8,128)(2,1)S(1)} %copy-done, f32[256,1792]{1,0:T(8,128)} %constant_dynamic-update-slice_fusion, s32[]{:T(128)S(6)} %select_n.253, f32[1024]{0:T(1024)S(1)} %copy-done.28, f32[256]{0:T(256)S(1)} %get-tuple-element.69, ...), kind=kOutput, calls=%fused_computation.25 | convolution fusion | flops 1076887552 | bytes 6821892 | tf_op jit(solution)/shard_map/dot_general | solution.py:297
  (142 shorter events, 25.2 us)
Async XLA Ops:
  0.0 306.9 %copy-start = (bf16[1024,1024]{1,0:T(8,128)(2,1)S(1)}, bf16[1024,1024]{1,0:T(8,128)(2,1)}, u32[]{:S(2)}) copy-start(bf16[1024,1024]{1,0:T(8,128)(2,1)} %param.20) | copy-start | bytes 6291460
  12.1 29.7 %copy-start.24 = (s32[1,1024]{1,0:T(1,128)S(1)}, s32[1,1024]{1,0:T(1,128)}, u32[]{:S(2)}) copy-start(s32[1,1024]{1,0:T(1,128)} %param.12) | copy-start | bytes 12292
  24.9 1.0 copy-start.3
  25.9 1.0 copy-start.4
  29.8 1.1 copy-start.11
  31.8 77.7 %collective-permute-start.16 = (bf16[2,4,4,128,128]{4,3,2,1,0:T(8,128)(2,1)}, bf16[2,4,4,128,128]{4,3,2,1,0:T(8,128)(2,1)}, u32[]{:S(2)}, u32[]{:S(2)}) collective-permute-start(bf16[2,4,4,128,128]{4,3,2,1,0:T(8,128)(2,1)} %get-tuple-element.36), channel_id=1, source_target_pairs={{0,4},{4,0},{8,12},{12,8},{16,20},{20,16},{24,28},{28,24},{32,36},... | collective-permute-start | bytes 3145736 | tf_op jit(solution)/shard_map/ppermute | solution.py:211
  41.9 70.6 %collective-permute-start.17 = (bf16[2,4,4,128,128]{4,3,2,1,0:T(8,128)(2,1)}, bf16[2,4,4,128,128]{4,3,2,1,0:T(8,128)(2,1)}, u32[]{:S(2)}, u32[]{:S(2)}) collective-permute-start(bf16[2,4,4,128,128]{4,3,2,1,0:T(8,128)(2,1)} %get-tuple-element.37), channel_id=1, source_target_pairs={{0,8},{4,36},{8,16},{12,44},{16,24},{20,52},{24,0},{28,60},{32,40}... | collective-permute-start | bytes 3145736 | tf_op jit(solution)/shard_map/ppermute | solution.py:211
  49.0 55.1 %collective-permute-start.1 = (bf16[256,1024]{1,0:T(8,128)(2,1)}, bf16[256,1024]{1,0:T(8,128)(2,1)}, u32[]{:S(2)}, u32[]{:S(2)}) collective-permute-start(bf16[256,1024]{1,0:T(8,128)(2,1)} %select_select_fusion.1), channel_id=1, source_target_pairs={{0,2},{1,3},{2,0},{3,1},{4,6},{5,7},{6,4},{7,5},{8,10},{9,11},{10,... | collective-permute-start | bytes 1572872 | tf_op jit(solution)/shard_map/ppermute | solution.py:226
  60.8 43.8 %collective-permute-start = (bf16[256,1024]{1,0:T(8,128)(2,1)}, bf16[256,1024]{1,0:T(8,128)(2,1)}, u32[]{:S(2)}, u32[]{:S(2)}) collective-permute-start(bf16[256,1024]{1,0:T(8,128)(2,1)} %select_select_fusion.2), channel_id=1, source_target_pairs={{0,1},{1,2},{2,3},{3,0},{4,5},{5,6},{6,7},{7,4},{8,9},{9,10},{10,1... | collective-permute-start | bytes 1572872 | tf_op jit(solution)/shard_map/ppermute | solution.py:226
  61.9 9.3 %copy-start.26 = (s32[4]{0:T(128)S(1)}, s32[4]{0:T(128)}, u32[]{:S(2)}) copy-start(s32[4]{0:T(128)} %constant.229.clone) | copy-start | bytes 52
  68.9 37.8 %collective-permute-start.2 = (bf16[256,1024]{1,0:T(8,128)(2,1)}, bf16[256,1024]{1,0:T(8,128)(2,1)}, u32[]{:S(2)}, u32[]{:S(2)}) collective-permute-start(bf16[256,1024]{1,0:T(8,128)(2,1)} %select_select_fusion), channel_id=1, source_target_pairs={{0,3},{1,0},{2,1},{3,2},{4,7},{5,4},{6,5},{7,6},{8,11},{9,8},{10,9... | collective-permute-start | bytes 1572872 | tf_op jit(solution)/shard_map/ppermute | solution.py:226
  72.3 5.1 %copy-start.25 = (s32[1,4,64]{2,1,0:T(4,128)S(1)}, s32[1,4,64]{2,1,0:T(4,128)}, u32[]{:S(2)}) copy-start(s32[1,4,64]{2,1,0:T(4,128)} %param.16) | copy-start | bytes 3076
  104.2 5.4 %copy-start.9 = (bf16[2,4,4,128,128]{4,3,2,1,0:T(8,128)(2,1)S(1)}, bf16[2,4,4,128,128]{4,3,2,1,0:T(8,128)(2,1)}, u32[]{:S(2)}) copy-start(bf16[2,4,4,128,128]{4,3,2,1,0:T(8,128)(2,1)} %copy-done.8) | copy-start | bytes 3145732
  104.2 8.3 %copy-start.7 = (bf16[2,4,4,128,128]{4,3,2,1,0:T(8,128)(2,1)S(1)}, bf16[2,4,4,128,128]{4,3,2,1,0:T(8,128)(2,1)}, u32[]{:S(2)}) copy-start(bf16[2,4,4,128,128]{4,3,2,1,0:T(8,128)(2,1)} %copy-done.6) | copy-start | bytes 3145732
  104.2 68.1 %copy-start.27 = (bf16[1024,256]{1,0:T(8,128)(2,1)S(1)}, bf16[1024,256]{1,0:T(8,128)(2,1)}, u32[]{:S(2)}) copy-start(bf16[1024,256]{1,0:T(8,128)(2,1)} %param.17) | copy-start | bytes 1572868
  104.2 38.2 %collective-permute-start.18 = (bf16[2,4,4,128,128]{4,3,2,1,0:T(8,128)(2,1)}, bf16[2,4,4,128,128]{4,3,2,1,0:T(8,128)(2,1)S(1)}, u32[]{:S(2)}, u32[]{:S(2)}) collective-permute-start(bf16[2,4,4,128,128]{4,3,2,1,0:T(8,128)(2,1)} %copy-done.12), channel_id=1, source_target_pairs={{0,36},{4,8},{8,44},{12,16},{16,52},{20,24},{24,60},{28,0},{32,68}... | collective-permute-start | bytes 3145736 | tf_op jit(solution)/shard_map/ppermute | solution.py:211
  104.7 38.7 %collective-permute-start.19 = (bf16[2,4,4,128,128]{4,3,2,1,0:T(8,128)(2,1)}, bf16[2,4,4,128,128]{4,3,2,1,0:T(8,128)(2,1)S(1)}, u32[]{:S(2)}, u32[]{:S(2)}) collective-permute-start(bf16[2,4,4,128,128]{4,3,2,1,0:T(8,128)(2,1)} %copy-done.11), channel_id=1, source_target_pairs={{0,16},{4,68},{8,24},{12,76},{16,0},{20,84},{24,8},{28,92},{32,48}... | collective-permute-start | bytes 3145736 | tf_op jit(solution)/shard_map/ppermute | solution.py:211
  106.7 39.1 %collective-permute-start.20 = (bf16[2,4,4,128,128]{4,3,2,1,0:T(8,128)(2,1)}, bf16[2,4,4,128,128]{4,3,2,1,0:T(8,128)(2,1)S(1)}, u32[]{:S(2)}, u32[]{:S(2)}) collective-permute-start(bf16[2,4,4,128,128]{4,3,2,1,0:T(8,128)(2,1)} %copy-done.10), channel_id=1, source_target_pairs={{0,68},{4,16},{8,76},{12,24},{16,84},{20,0},{24,92},{28,8},{32,100... | collective-permute-start | bytes 3145736 | tf_op jit(solution)/shard_map/ppermute | solution.py:211
  109.5 64.3 %copy-start.23 = (bf16[256,1024]{1,0:T(8,128)(2,1)}, bf16[256,1024]{1,0:T(8,128)(2,1)S(1)}, u32[]{:S(2)}) copy-start(bf16[256,1024]{1,0:T(8,128)(2,1)S(1)} %fusion.16) | copy-start | bytes 1572868
  109.6 64.3 %collective-permute-start.21 = (bf16[2,4,4,128,128]{4,3,2,1,0:T(8,128)(2,1)S(1)}, bf16[2,4,4,128,128]{4,3,2,1,0:T(8,128)(2,1)S(1)}, u32[]{:S(2)}, u32[]{:S(2)}) collective-permute-start(bf16[2,4,4,128,128]{4,3,2,1,0:T(8,128)(2,1)S(1)} %copy-done.9), channel_id=1, source_target_pairs={{0,24},{4,100},{8,0},{12,108},{16,8},{20,116},{24,16},{28,124},{32... | collective-permute-start | bytes 3145736 | tf_op jit(solution)/shard_map/ppermute | solution.py:211
  112.4 62.7 %collective-permute-start.22 = (bf16[2,4,4,128,128]{4,3,2,1,0:T(8,128)(2,1)S(1)}, bf16[2,4,4,128,128]{4,3,2,1,0:T(8,128)(2,1)S(1)}, u32[]{:S(2)}, u32[]{:S(2)}) collective-permute-start(bf16[2,4,4,128,128]{4,3,2,1,0:T(8,128)(2,1)S(1)} %copy-done.7), channel_id=1, source_target_pairs={{0,100},{4,24},{8,108},{12,0},{16,116},{20,8},{24,124},{28,16},{32... | collective-permute-start | bytes 3145736 | tf_op jit(solution)/shard_map/ppermute | solution.py:211
  142.4 1.0 copy-start.13
  143.4 26.6 %collective-permute-start.3 = (bf16[256,1024]{1,0:T(8,128)(2,1)S(1)}, bf16[256,1024]{1,0:T(8,128)(2,1)S(1)}, u32[]{:S(2)}, u32[]{:S(2)}) collective-permute-start(bf16[256,1024]{1,0:T(8,128)(2,1)S(1)} %fusion.16), channel_id=1, source_target_pairs={{0,1},{1,2},{2,3},{3,0},{4,5},{5,6},{6,7},{7,4},{8,9},{9,10},{10,1... | collective-permute-start | bytes 1572872 | tf_op jit(solution)/shard_map/ppermute | solution.py:227
  144.4 25.6 %collective-permute-start.4 = (bf16[256,1024]{1,0:T(8,128)(2,1)S(1)}, bf16[256,1024]{1,0:T(8,128)(2,1)S(1)}, u32[]{:S(2)}, u32[]{:S(2)}) collective-permute-start(bf16[256,1024]{1,0:T(8,128)(2,1)S(1)} %fusion.16), channel_id=1, source_target_pairs={{0,2},{1,3},{2,0},{3,1},{4,6},{5,7},{6,4},{7,5},{8,10},{9,11},{10,... | collective-permute-start | bytes 1572872 | tf_op jit(solution)/shard_map/ppermute | solution.py:227
  146.8 25.5 %collective-permute-start.5 = (bf16[256,1024]{1,0:T(8,128)(2,1)S(1)}, bf16[256,1024]{1,0:T(8,128)(2,1)S(1)}, u32[]{:S(2)}, u32[]{:S(2)}) collective-permute-start(bf16[256,1024]{1,0:T(8,128)(2,1)S(1)} %fusion.16), channel_id=1, source_target_pairs={{0,3},{1,0},{2,1},{3,2},{4,7},{5,4},{6,5},{7,6},{8,11},{9,8},{10,9... | collective-permute-start | bytes 1572872 | tf_op jit(solution)/shard_map/ppermute | solution.py:227
  170.0 27.8 %collective-permute-start.10 = (bf16[2,4,4,128,128]{4,3,2,1,0:T(8,128)(2,1)}, bf16[2,4,4,128,128]{4,3,2,1,0:T(8,128)(2,1)}, u32[]{:S(2)}, u32[]{:S(2)}) collective-permute-start(bf16[2,4,4,128,128]{4,3,2,1,0:T(8,128)(2,1)} %get-tuple-element.30), channel_id=1, source_target_pairs={{0,16},{4,68},{8,24},{12,76},{16,0},{20,84},{24,8},{28,92},{32,48}... | collective-permute-start | bytes 3145736 | tf_op jit(solution)/shard_map/ppermute | solution.py:211
  170.0 27.8 %collective-permute-start.11 = (bf16[2,4,4,128,128]{4,3,2,1,0:T(8,128)(2,1)}, bf16[2,4,4,128,128]{4,3,2,1,0:T(8,128)(2,1)}, u32[]{:S(2)}, u32[]{:S(2)}) collective-permute-start(bf16[2,4,4,128,128]{4,3,2,1,0:T(8,128)(2,1)} %get-tuple-element.31), channel_id=1, source_target_pairs={{0,68},{4,16},{8,76},{12,24},{16,84},{20,0},{24,92},{28,8},{32,100... | collective-permute-start | bytes 3145736 | tf_op jit(solution)/shard_map/ppermute | solution.py:211
  172.3 36.4 %collective-permute-start.12 = (bf16[2,4,4,128,128]{4,3,2,1,0:T(8,128)(2,1)}, bf16[2,4,4,128,128]{4,3,2,1,0:T(8,128)(2,1)}, u32[]{:S(2)}, u32[]{:S(2)}) collective-permute-start(bf16[2,4,4,128,128]{4,3,2,1,0:T(8,128)(2,1)} %get-tuple-element.32), channel_id=1, source_target_pairs={{0,24},{4,100},{8,0},{12,108},{16,8},{20,116},{24,16},{28,124},{32... | collective-permute-start | bytes 3145736 | tf_op jit(solution)/shard_map/ppermute | solution.py:211
  174.8 33.9 %collective-permute-start.14 = (bf16[1024,256]{1,0:T(8,128)(2,1)}, bf16[1024,256]{1,0:T(8,128)(2,1)}, u32[]{:S(2)}, u32[]{:S(2)}) collective-permute-start(bf16[1024,256]{1,0:T(8,128)(2,1)} %fusion.10.rest_1_), channel_id=1, source_target_pairs={{0,64},{4,20},{8,72},{12,28},{16,80},{20,4},{24,88},{28,12},{32,96... | collective-permute-start | bytes 1572872 | tf_op jit(solution)/shard_map/ppermute | solution.py:234
  176.1 34.4 %collective-permute-start.15 = (bf16[1024,256]{1,0:T(8,128)(2,1)}, bf16[1024,256]{1,0:T(8,128)(2,1)}, u32[]{:S(2)}, u32[]{:S(2)}) collective-permute-start(bf16[1024,256]{1,0:T(8,128)(2,1)} %fusion.10.rest_1_), channel_id=1, source_target_pairs={{0,96},{4,28},{8,104},{12,4},{16,112},{20,12},{24,120},{28,20},{32... | collective-permute-start | bytes 1572872 | tf_op jit(solution)/shard_map/ppermute | solution.py:234
  197.7 48.2 %collective-permute-start.13 = (bf16[2,4,4,128,128]{4,3,2,1,0:T(8,128)(2,1)}, bf16[2,4,4,128,128]{4,3,2,1,0:T(8,128)(2,1)S(1)}, u32[]{:S(2)}, u32[]{:S(2)}) collective-permute-start(bf16[2,4,4,128,128]{4,3,2,1,0:T(8,128)(2,1)} %get-tuple-element.33), channel_id=1, source_target_pairs={{0,100},{4,24},{8,108},{12,0},{16,116},{20,8},{24,124},{28,16},{32... | collective-permute-start | bytes 3145736 | tf_op jit(solution)/shard_map/ppermute | solution.py:211
  197.7 48.3 %collective-permute-start.7 = (bf16[2,4,4,128,128]{4,3,2,1,0:T(8,128)(2,1)}, bf16[2,4,4,128,128]{4,3,2,1,0:T(8,128)(2,1)S(1)}, u32[]{:S(2)}, u32[]{:S(2)}) collective-permute-start(bf16[2,4,4,128,128]{4,3,2,1,0:T(8,128)(2,1)} %copy-done.3), channel_id=1, source_target_pairs={{0,4},{4,0},{8,12},{12,8},{16,20},{20,16},{24,28},{28,24},{32,36},... | collective-permute-start | bytes 3145736 | tf_op jit(solution)/shard_map/ppermute | solution.py:211
  208.7 43.3 %collective-permute-start.8 = (bf16[2,4,4,128,128]{4,3,2,1,0:T(8,128)(2,1)}, bf16[2,4,4,128,128]{4,3,2,1,0:T(8,128)(2,1)S(1)}, u32[]{:S(2)}, u32[]{:S(2)}) collective-permute-start(bf16[2,4,4,128,128]{4,3,2,1,0:T(8,128)(2,1)} %copy-done.2), channel_id=1, source_target_pairs={{0,8},{4,36},{8,16},{12,44},{16,24},{20,52},{24,0},{28,60},{32,40}... | collective-permute-start | bytes 3145736 | tf_op jit(solution)/shard_map/ppermute | solution.py:211
  208.8 43.3 %collective-permute-start.9 = (bf16[2,4,4,128,128]{4,3,2,1,0:T(8,128)(2,1)}, bf16[2,4,4,128,128]{4,3,2,1,0:T(8,128)(2,1)S(1)}, u32[]{:S(2)}, u32[]{:S(2)}) collective-permute-start(bf16[2,4,4,128,128]{4,3,2,1,0:T(8,128)(2,1)} %copy-done.1), channel_id=1, source_target_pairs={{0,36},{4,8},{8,44},{12,16},{16,52},{20,24},{24,60},{28,0},{32,68}... | collective-permute-start | bytes 3145736 | tf_op jit(solution)/shard_map/ppermute | solution.py:211
  210.5 41.5 %collective-permute-start.6 = (bf16[1024,256]{1,0:T(8,128)(2,1)}, bf16[1024,256]{1,0:T(8,128)(2,1)S(1)}, u32[]{:S(2)}, u32[]{:S(2)}) collective-permute-start(bf16[1024,256]{1,0:T(8,128)(2,1)} %fusion.10.rest_1_), channel_id=1, source_target_pairs={{0,32},{4,12},{8,40},{12,20},{16,48},{20,28},{24,56},{28,4},{32,64... | collective-permute-start | bytes 1572872 | tf_op jit(solution)/shard_map/ppermute | solution.py:234
  214.5 1.2 copy-start.5
  215.7 1.2 copy-start.14
  216.9 1.2 copy-start.16
  218.1 1.2 copy-start.18
  219.4 1.2 copy-start.20
  220.6 1.2 copy-start.22
  245.9 31.1 %collective-permute-start.23 = (bf16[1024,256]{1,0:T(8,128)(2,1)S(1)}, bf16[1024,256]{1,0:T(8,128)(2,1)S(1)}, u32[]{:S(2)}, u32[]{:S(2)}) collective-permute-start(bf16[1024,256]{1,0:T(8,128)(2,1)S(1)} %get-tuple-element.43), channel_id=1, source_target_pairs={{0,32},{4,12},{8,40},{12,20},{16,48},{20,28},{24,56},{28,4},{32,64... | collective-permute-start | bytes 1572872 | tf_op jit(solution)/shard_map/ppermute | solution.py:283
  246.0 31.0 %collective-permute-start.24 = (bf16[1024,256]{1,0:T(8,128)(2,1)S(1)}, bf16[1024,256]{1,0:T(8,128)(2,1)S(1)}, u32[]{:S(2)}, u32[]{:S(2)}) collective-permute-start(bf16[1024,256]{1,0:T(8,128)(2,1)S(1)} %get-tuple-element.44), channel_id=1, source_target_pairs={{0,64},{4,20},{8,72},{12,28},{16,80},{20,4},{24,88},{28,12},{32,96... | collective-permute-start | bytes 1572872 | tf_op jit(solution)/shard_map/ppermute | solution.py:283
  276.9 9.2 %collective-permute-start.25 = (bf16[1024,256]{1,0:T(8,128)(2,1)S(1)}, bf16[1024,256]{1,0:T(8,128)(2,1)S(1)}, u32[]{:S(2)}, u32[]{:S(2)}) collective-permute-start(bf16[1024,256]{1,0:T(8,128)(2,1)S(1)} %get-tuple-element.45), channel_id=1, source_target_pairs={{0,96},{4,28},{8,104},{12,4},{16,112},{20,12},{24,120},{28,20},{32... | collective-permute-start | bytes 1572872 | tf_op jit(solution)/shard_map/ppermute | solution.py:283
  287.4 8.7 %collective-permute-start.26 = (f32[256,256]{1,0:T(8,128)}, f32[256,256]{1,0:T(8,128)S(1)}, u32[]{:S(2)}, u32[]{:S(2)}) collective-permute-start(f32[256,256]{1,0:T(8,128)} %get-tuple-element.59), channel_id=1, source_target_pairs={{0,3},{1,0},{2,1},{3,2},{4,7},{5,4},{6,5},{7,6},{8,11},{9,8},{10,9... | collective-permute-start | bytes 786440 | tf_op jit(solution)/shard_map/ppermute | solution.py:288
  287.4 10.4 %collective-permute-start.27 = (f32[256,256]{1,0:T(8,128)}, f32[256,256]{1,0:T(8,128)}, u32[]{:S(2)}, u32[]{:S(2)}) collective-permute-start(f32[256,256]{1,0:T(8,128)} %get-tuple-element.58), channel_id=1, source_target_pairs={{0,2},{1,3},{2,0},{3,1},{4,6},{5,7},{6,4},{7,5},{8,10},{9,11},{10,... | collective-permute-start | bytes 786440 | tf_op jit(solution)/shard_map/ppermute | solution.py:288
  287.4 13.1 %collective-permute-start.28 = (f32[256,256]{1,0:T(8,128)}, f32[256,256]{1,0:T(8,128)}, u32[]{:S(2)}, u32[]{:S(2)}) collective-permute-start(f32[256,256]{1,0:T(8,128)} %get-tuple-element.56), channel_id=1, source_target_pairs={{0,1},{1,2},{2,3},{3,0},{4,5},{5,6},{6,7},{7,4},{8,9},{9,10},{10,1... | collective-permute-start | bytes 786440 | tf_op jit(solution)/shard_map/ppermute | solution.py:288
  296.1 10.8 %copy-start.28 = (f32[1024]{0:T(1024)S(1)}, f32[1024]{0:T(1024)}, u32[]{:S(2)}) copy-start(f32[1024]{0:T(1024)} %param.19) | copy-start | bytes 12292
  (10 other events, 9.7 us)

commit v2 on v1

v2 whole, which is shorter than its diff:
```python
import functools
import jax
import jax.numpy as jnp
from jax import lax
from jax.experimental import pallas as pl
from jax.experimental.pallas import tpu as pltpu
from jax.sharding import PartitionSpec as P

DH = 64
BLK = 128
SLOT = 4
CB = 256
RING = 4
SOURCES = 8
GROUP = 4
HOPS = (2, 1, 3)

norm_eps = 1e-05
MESH = pl.DeviceIdType.MESH


def at(x, y, core):
    return (lax.rem(x + 2 * RING, RING) * RING + lax.rem(y + 2 * RING, RING)) * 2 + core


def place():
    me = lax.axis_index("cache")
    core = lax.rem(me, 2)
    y = lax.rem(lax.div(me, 2), RING)
    x = lax.div(me, 2 * RING)
    return x, y, core


def ring_peer(k):
    x, y, core = place()
    return jnp.where(core == 0, at(x + k, y, 0), at(x, y + k, 1))


def kv_dest(i):
    x, y, core = place()
    j, s = lax.div(i, 2), lax.rem(i, 2)
    return jnp.where(core == s, at(x, y + j, 0), at(x + j, y, 1))


def kv_source(i):
    x, y, core = place()
    j, s = lax.div(i, 2), lax.rem(i, 2)
    return jnp.where(core == 0, at(x, y - j, s), at(x - j, y, 1 - s))


def kv_request(i, k):
    x, y, core = place()
    j, s = lax.div(i, 2), lax.rem(i, 2)
    return jnp.where(core == s, at(x + k, y + j, 0), at(x + j, y + k, 1))


def ring_pairs(k):
    pairs = []
    for x in range(RING):
        for y in range(RING):
            here = (x * RING + y) * 2
            pairs.append((here, ((x + k) % RING * RING + y) * 2))
            pairs.append((here + 1, (x * RING + (y + k) % RING) * 2 + 1))
    return pairs


def gather_kernel(
    zs, send_ref, ids_ref, kv_ref, table_ref, wq_ref, wg_ref,
    recv_ref, q_ref, embedded_ref, gate_ref,
    stage, turn, parts, parts_in, chunks, queries,
    kv_out, kv_in, z1_out, z1_in, z2_out, z2_in, q_out, q_in, own_sem,
):
    z = lax.axis_index("item")
    rows = embedded_ref.shape[0]
    peer_z = lambda d: lax.rem(z + d + zs, zs)

    barrier = pltpu.get_barrier_semaphore()
    for i in range(1, SOURCES):
        pl.semaphore_signal(barrier, inc=1, device_id={"cache": kv_source(i)}, device_id_type=MESH)
    for k in HOPS:
        pl.semaphore_signal(barrier, inc=1, device_id={"cache": ring_peer(k)}, device_id_type=MESH)
        pl.semaphore_signal(barrier, inc=1, device_id={"item": peer_z(k)}, device_id_type=MESH)
    pl.semaphore_wait(barrier, SOURCES - 1 + 2 * len(HOPS))

    side = turn.shape[0]
    heads = side // BLK
    to = lax.broadcasted_iota(jnp.int32, turn.shape, 0)
    of = lax.broadcasted_iota(jnp.int32, turn.shape, 1)
    turn[...] = jnp.where(
        of == lax.rem(to, BLK) * heads + lax.div(to, BLK), 1.0, 0.0
    ).astype(turn.dtype)

    def kv_copy(i, k):
        return pltpu.make_async_remote_copy(
            src_ref=stage.at[i, k],
            dst_ref=recv_ref.at[i, k],
            send_sem=kv_out.at[i * RING + k],
            recv_sem=kv_in.at[i * RING + k],
            device_id={"cache": kv_dest(i)},
            device_id_type=MESH,
        )

    def own_copy(k):
        return pltpu.make_async_copy(stage.at[0, k], recv_ref.at[0, k], kv_out.at[k])

    def send_blocks(k):
        def step(n, carry):
            i = lax.rem(n + 2, SOURCES)
            request = kv_request(i, k)
            for slot in range(SLOT):
                block = kv_ref[send_ref[request * SLOT + slot]]
                stage[i, k, slot] = jnp.dot(
                    turn[...], block, preferred_element_type=jnp.float32
                ).astype(stage.dtype)

            @pl.when(i == 0)
            def _():
                own_copy(k).start()

            @pl.when(i != 0)
            def _():
                kv_copy(i, k).start()

            return carry

        lax.fori_loop(0, SOURCES, step, 0)

    def z1_copy(d):
        return pltpu.make_async_remote_copy(
            src_ref=parts.at[d],
            dst_ref=parts_in.at[d - 1],
            send_sem=z1_out.at[d - 1],
            recv_sem=z1_in.at[d - 1],
            device_id={"item": peer_z(d)},
            device_id_type=MESH,
        )

    def z2_copy(d):
        return pltpu.make_async_remote_copy(
            src_ref=chunks.at[0],
            dst_ref=chunks.at[d],
            send_sem=z2_out.at[d - 1],
            recv_sem=z2_in.at[d - 1],
            device_id={"item": peer_z(d)},
            device_id_type=MESH,
        )

    def q_copy(k):
        return pltpu.make_async_remote_copy(
            src_ref=queries,
            dst_ref=q_ref.at[k],
            send_sem=q_out.at[k - 1],
            recv_sem=q_in.at[k - 1],
            device_id={"cache": ring_peer(-k)},
            device_id_type=MESH,
        )

    send_blocks(2)

    for d in HOPS + (0,):
        ids = ids_ref[d * rows : (d + 1) * rows, :]
        hot = ids == lax.broadcasted_iota(jnp.int32, (rows, table_ref.shape[0]), 1)
        parts[d] = jnp.dot(
            jnp.where(hot, 1.0, 0.0).astype(table_ref.dtype),
            table_ref[...],
            preferred_element_type=jnp.float32,
        ).astype(parts.dtype)
        if d != 0:
            z1_copy(d).start()

    send_blocks(1)

    for d in HOPS:
        z1_copy(d).wait_recv()
    embedded = parts[0] + parts_in[0] + parts_in[1] + parts_in[2]
    chunks[0] = embedded
    for d in HOPS:
        z2_copy(d).start()
    embedded_ref[...] = embedded

    send_blocks(3)
    send_blocks(0)

    def silu(v):
        return v * jax.nn.sigmoid(v)

    gate_ref[...] = silu(jnp.dot(embedded, wg_ref[...], preferred_element_type=jnp.float32))
    scale = 0.5 * DH ** (-0.5)
    for d in (0,) + HOPS:
        if d != 0:
            z2_copy(d).wait_recv()
        queries[d * rows : (d + 1) * rows, :] = (
            silu(jnp.dot(chunks[d], wq_ref[...], preferred_element_type=jnp.float32)).astype(
                queries.dtype
            )
            * jnp.asarray(scale, queries.dtype)
        )
    for k in HOPS:
        q_copy(k).start()
    own_q = pltpu.make_async_copy(queries, q_ref.at[0], own_sem.at[0])
    own_q.start()

    for d in HOPS:
        z1_copy(d).wait_send()
        z2_copy(d).wait_send()

    def drain(n, carry):
        i, k = lax.div(n, RING), lax.rem(n, RING)

        @pl.when(i == 0)
        def _():
            own_copy(k).wait()

        @pl.when(i != 0)
        def _():
            kv_copy(i, k).wait()

        return carry

    lax.fori_loop(0, SOURCES * RING, drain, 0)
    own_q.wait()
    for k in HOPS:
        q_copy(k).wait()


def gather(zs, send, ids, kv, table, w_query, w_gate):
    smem = pl.BlockSpec(memory_space=pltpu.SMEM)
    vmem = pl.BlockSpec(memory_space=pltpu.VMEM)
    hbm = pl.BlockSpec(memory_space=pl.ANY)
    rows = ids.shape[0] // zs
    width = table.shape[1]
    part = w_query.shape[1]
    dma = pltpu.SemaphoreType.DMA
    moved = (SOURCES, RING, SLOT) + kv.shape[1:]
    return pl.pallas_call(
        functools.partial(gather_kernel, zs),
        out_shape=[
            jax.ShapeDtypeStruct(moved, kv.dtype),
            jax.ShapeDtypeStruct((RING, zs * rows, part), kv.dtype),
            jax.ShapeDtypeStruct((rows, width), kv.dtype),
            jax.ShapeDtypeStruct((rows, width), jnp.float32),
        ],
        in_specs=[smem, vmem, vmem, vmem, vmem, vmem],
        out_specs=[hbm, hbm, vmem, vmem],
        scratch_shapes=[
            pltpu.VMEM(moved, kv.dtype),
            pltpu.VMEM((kv.shape[1], kv.shape[1]), kv.dtype),
            pltpu.VMEM((zs, rows, width), kv.dtype),
            pltpu.VMEM((zs - 1, rows, width), kv.dtype),
            pltpu.VMEM((zs, rows, width), kv.dtype),
            pltpu.VMEM((zs * rows, part), kv.dtype),
            dma((SOURCES * RING,)),
            dma((SOURCES * RING,)),
            dma((zs - 1,)),
            dma((zs - 1,)),
            dma((zs - 1,)),
            dma((zs - 1,)),
            dma((RING - 1,)),
            dma((RING - 1,)),
            dma((1,)),
        ],
        compiler_params=pltpu.CompilerParams(
            collective_id=0, has_side_effects=True, vmem_limit_bytes=56 * 2**20
        ),
        name="gather",
    )(send, ids, kv, table, w_query, w_gate)


def attend_kernel(cblks, heads, count_ref, list_ref, q_ref, kv_ref, o_ref, held, queries, acc, sems):
    nk = q_ref.shape[0]
    entries = SOURCES * SLOT
    stride = entries + GROUP

    def copy(k, i):
        return pltpu.make_async_copy(
            kv_ref.at[i, k], held.at[k, pl.ds(i * SLOT, SLOT)], sems.at[k * SOURCES + i]
        )

    for k in range(nk):
        for i in range(SOURCES):
            copy(k, i).start()
        held[k, entries] = jnp.zeros(held.shape[2:], held.dtype)
    for k in range(nk):
        for h in range(heads):
            queries[h] = q_ref[k, :, h * DH : (h + 1) * DH]
        for i in range(SOURCES):
            copy(k, i).wait()

        def one_cblk(c, carry, k=k):
            rows = pl.ds(pl.multiple_of(c * CB, CB), CB)
            acc[...] = jnp.zeros_like(acc)

            def group(g, carry):
                base = (k * cblks + c) * stride + g * GROUP
                ids = [list_ref[base + i] for i in range(GROUP)]
                kvs = [
                    jnp.concatenate([held[k, e, h] for e in ids], axis=0) for h in range(heads)
                ]
                halves = [
                    lax.dot_general(
                        queries[h, rows, :],
                        kvs[h][:, :DH],
                        (((1,), (1,)), ((), ())),
                        preferred_element_type=jnp.float32,
                    )
                    for h in range(heads)
                ]
                weights = [(s + s * jnp.tanh(s)).astype(jnp.bfloat16) for s in halves]
                for h in range(heads):
                    acc[h] += jnp.dot(weights[h], kvs[h], preferred_element_type=jnp.float32)
                return carry

            groups = (count_ref[k * cblks + c] + GROUP - 1) // GROUP
            lax.fori_loop(0, groups, group, 0)
            o_ref[k, rows, :] = jnp.concatenate(
                [acc[h][:, DH:] for h in range(heads)], axis=1
            ).astype(o_ref.dtype)
            return carry

        lax.fori_loop(0, cblks, one_cblk, 0)


def attend(counts, lists, qs, kvs):
    nk, rows, width = qs.shape
    heads = width // DH
    cblks = rows // CB
    smem = pl.BlockSpec(memory_space=pltpu.SMEM)
    vmem = pl.BlockSpec(memory_space=pltpu.VMEM)
    hbm = pl.BlockSpec(memory_space=pl.ANY)
    entries = SOURCES * SLOT
    work = nk * cblks * heads * CB * BLK * entries
    return pl.pallas_call(
        functools.partial(attend_kernel, cblks, heads),
        out_shape=jax.ShapeDtypeStruct(qs.shape, qs.dtype),
        in_specs=[smem, smem, vmem, hbm],
        out_specs=vmem,
        scratch_shapes=[
            pltpu.VMEM((nk, entries + 1, heads, BLK, 2 * DH), qs.dtype),
            pltpu.VMEM((heads, rows, DH), qs.dtype),
            pltpu.VMEM((heads, CB, 2 * DH), jnp.float32),
            pltpu.SemaphoreType.DMA((nk * SOURCES,)),
        ],
        compiler_params=pltpu.CompilerParams(vmem_limit_bytes=48 * 2**20),
        cost_estimate=pl.CostEstimate(
            flops=16 * work * DH, bytes_accessed=nk * 6 * 2**20, transcendentals=work
        ),
        name="attend",
    )(counts, lists, qs, kvs)


def finish_kernel(
    zs, o_ref, embedded_ref, gate_ref, gain_ref, w_ref, out_ref,
    sums_in, pieces, pieces_in, o_out, o_in, z_out, z_in,
):
    z = lax.axis_index("item")
    peer_z = lambda d: lax.rem(z + d + zs, zs)
    rows, width = out_ref.shape
    part = width // zs

    barrier = pltpu.get_barrier_semaphore()
    for k in HOPS:
        pl.semaphore_signal(barrier, inc=1, device_id={"cache": ring_peer(k)}, device_id_type=MESH)
        pl.semaphore_signal(barrier, inc=1, device_id={"item": peer_z(k)}, device_id_type=MESH)
    pl.semaphore_wait(barrier, 2 * len(HOPS))

    def o_copy(i, k):
        at_rows = pl.ds(i * rows, rows)
        return pltpu.make_async_remote_copy(
            src_ref=o_ref.at[k, at_rows],
            dst_ref=sums_in.at[k - 1, at_rows],
            send_sem=o_out.at[i * (RING - 1) + k - 1],
            recv_sem=o_in.at[i * (RING - 1) + k - 1],
            device_id={"cache": ring_peer(k)},
            device_id_type=MESH,
        )

    def z_copy(i):
        return pltpu.make_async_remote_copy(
            src_ref=pieces.at[i],
            dst_ref=pieces_in.at[i - 1],
            send_sem=z_out.at[i - 1],
            recv_sem=z_in.at[i - 1],
            device_id={"item": peer_z(-i)},
            device_id_type=MESH,
        )

    for i in HOPS + (0,):
        for k in HOPS:
            o_copy(i, k).start()
    for i in HOPS + (0,):
        total = o_ref[0, i * rows : (i + 1) * rows, :].astype(jnp.float32)
        for k in HOPS:
            o_copy(i, k).wait_recv()
            total += sums_in[k - 1, i * rows : (i + 1) * rows, :].astype(jnp.float32)
        pieces[i] = total
        if i != 0:
            z_copy(i).start()
    for i in HOPS:
        z_copy(i).wait_recv()
    attended = [pieces[0]] + [pieces_in[i - 1] for i in range(1, zs)]
    row_mean = sum(jnp.sum(a, axis=1, keepdims=True) for a in attended) / width
    row_square = sum(jnp.sum(a * a, axis=1, keepdims=True) for a in attended) / width
    scale = lax.rsqrt(row_square - row_mean * row_mean + norm_eps)
    total = embedded_ref[...].astype(jnp.float32)
    for i, a in enumerate(attended):
        cols = pl.ds(pl.multiple_of(peer_z(i) * part, part), part)
        hidden = (a - row_mean) * scale * gain_ref[:, cols] * gate_ref[:, cols]
        total += jnp.dot(
            hidden.astype(jnp.bfloat16), w_ref[cols, :], preferred_element_type=jnp.float32
        )
    out_ref[...] = total.astype(out_ref.dtype)
    for i in HOPS:
        z_copy(i).wait_send()
    for i in range(zs):
        for k in HOPS:
            o_copy(i, k).wait_send()


def finish(zs, sums, embedded, gate_act, norm_gain, w_out):
    vmem = pl.BlockSpec(memory_space=pltpu.VMEM)
    rows, width = embedded.shape
    dma = pltpu.SemaphoreType.DMA
    return pl.pallas_call(
        functools.partial(finish_kernel, zs),
        out_shape=jax.ShapeDtypeStruct(embedded.shape, embedded.dtype),
        in_specs=[vmem] * 5,
        out_specs=vmem,
        scratch_shapes=[
            pltpu.VMEM((RING - 1,) + sums.shape[1:], sums.dtype),
            pltpu.VMEM((zs, rows, width // zs), jnp.float32),
            pltpu.VMEM((zs - 1, rows, width // zs), jnp.float32),
            dma((zs * (RING - 1),)),
            dma((zs * (RING - 1),)),
            dma((zs - 1,)),
            dma((zs - 1,)),
        ],
        compiler_params=pltpu.CompilerParams(
            collective_id=1, has_side_effects=True, vmem_limit_bytes=32 * 2**20
        ),
        name="finish",
    )(sums, embedded, gate_act, norm_gain[None, :], w_out)


def on_device(
    cand_items, item_table, kv_cache, hist_blocks, pattern, w_query, w_gate, norm_gain, w_out
):
    zs = lax.axis_size("item")
    z = lax.axis_index("item")
    me = lax.axis_index("cache")
    blocks_here = kv_cache.shape[0]
    list_len = hist_blocks.shape[1]
    item_ids = cand_items[0]
    rows_per = item_ids.shape[0] // zs

    owner_of = hist_blocks // blocks_here
    local_of = hist_blocks % blocks_here
    same_owner = owner_of[:, :, None] == owner_of[:, None, :]
    positions = jnp.arange(list_len)
    earlier = positions[None, :] < positions[:, None]
    slot_rank = jnp.sum(same_owner & earlier[None], axis=2)
    slots = jnp.arange(SLOT)
    selected = (owner_of == me)[:, None, :] & (slot_rank[:, None, :] == slots[None, :, None])
    send = jnp.sum(jnp.where(selected, local_of[:, None, :], 0), axis=2)

    turned = lax.dynamic_slice_in_dim(
        jnp.concatenate([item_ids, item_ids]), z * rows_per, item_ids.shape[0], 0
    )
    local_ids = (turned - z * item_table.shape[0])[:, None]
    kv_rows = kv_cache.reshape(blocks_here, -1, kv_cache.shape[3])
    moved, queries, embedded, gate_act = gather(
        zs, send.reshape(-1).astype(jnp.int32), local_ids, kv_rows, item_table, w_query, w_gate
    )
    moved = moved.reshape(moved.shape[:3] + (-1, BLK, 2 * DH))

    ks = jnp.arange(RING)
    request = jnp.stack([ring_peer(k) for k in range(RING)])
    sources = jnp.arange(SOURCES)
    owner_idx = jnp.stack([kv_source(i) for i in range(SOURCES)])
    owner_k = owner_of[request]
    rank_k = slot_rank[request]
    rotation = (z - jnp.arange(zs)) % zs
    pattern_of = [pattern[0]] + [
        lax.ppermute(pattern[0], "cache", ring_pairs(-k)) for k in range(1, RING)
    ]
    pattern_k = jnp.stack(pattern_of)[:, rotation]
    entry_of = jnp.sum(
        jnp.where(owner_k[:, None, :] == owner_idx[None, :, None], sources[None, :, None] + 1, 0), axis=1
    ) - 1
    entry_of = jnp.where(entry_of >= 0, entry_of * SLOT + rank_k, -1)
    wanted = (pattern_k != 0) & (entry_of >= 0)[:, None, :]
    before = jnp.sum(
        (wanted[:, :, None, :] & earlier[None, None]).astype(jnp.int32), axis=3
    )
    entries = SOURCES * SLOT
    places = jnp.arange(entries + GROUP)
    lists = entries + jnp.sum(
        jnp.where(
            wanted[:, :, None, :] & (before[:, :, None, :] == places[None, None, :, None]),
            entry_of[:, None, None, :] - entries,
            0,
        ),
        axis=3,
    )
    counts = jnp.sum(wanted.astype(jnp.int32), axis=2)
    sums = attend(
        counts.reshape(-1).astype(jnp.int32), lists.reshape(-1).astype(jnp.int32), queries, moved
    )
    return finish(zs, sums, embedded, gate_act, norm_gain, w_out)[None]


def solution(mesh):
    placed = (
        P("cache", None),
        P("item", None),
        P("cache", None, "item", None),
        P(),
        P("cache", None, None),
        P(None, "item"),
        P(),
        P(),
        P(),
    )
    return jax.shard_map(
        on_device, mesh=mesh, in_specs=placed, out_specs=P("cache", "item", None), check_vma=False
    )
```

time: 313 us -> 217 us (0.69)
  Pallas kernels: 59.8 us -> 194 us
  waiting for transfers between devices: 97.6 us -> 0.01 us
  local copies, waits for them, and re-layouts: 62.1 us -> 6.37 us
  starting transfers between devices: 44.5 us -> 5.74 us
  blocking collectives: 25.6 us -> 0 us
  other arithmetic: 15.4 us -> 6.66 us
  matrix products: 5.9 us -> 0 us
    pallas_call x3, Pallas kernels: 59.8 us -> 194 us  [the longest x1 117 us: gather(): pl.pallas_call(functools.partial(gather_kernel, zs), out_shape=[jax.Shape...]
    ppermute x29 -> x3, waiting for transfers between devices: 97.6 us -> 0.01 us  [on_device(): lax.ppermute(pattern[0], 'cache', ring_pairs(-k))]
    ppermute x29 -> x3, starting transfers between devices: 44.5 us -> 5.74 us  [on_device(): lax.ppermute(pattern[0], 'cache', ring_pairs(-k))]
    unnamed x64 -> x14, local copies, waits for them, and re-layouts: 35.8 us -> 2.5 us
    all_gather x1 -> x0, blocking collectives: 25.6 us -> none  [on_device(): pattern_all = lax.all_gather(pattern[0], 'cache')]
    gather x7 -> x1, local copies, waits for them, and re-layouts: 21.5 us -> 0.57 us  [on_device(): pattern_k = jnp.stack(pattern_of)[:, rotation]]
    dot_general x2 -> x0, matrix products: 5.9 us -> none  [the longest x1 4.35 us: on_device(): projected = jnp.dot(hidden, w_out, preferred_element_type=jnp.float32)]
    select_n x8 -> x3, other arithmetic: 5.99 us -> 0.82 us  [the longest x1 0.73 us: on_device(): local_of = hist_blocks % blocks_here]
  transfers between devices with their start and end apart: 29 -> 3, of which waited for: 8 -> 0; matrix products, arithmetic and copies ran while one was open for 12% -> 3% of each run, Pallas kernels for 16% -> 55%
where the time goes in v2:
time: 217 us; the launch traced here: 213 us
  Pallas kernels  194 us (89%)
  other arithmetic  6.66 us (3%)
  local copies, waits for them, and re-layouts  6.37 us (3%)
  starting transfers between devices  5.74 us (3%)
    pallas_call x1, Pallas kernels, gather(): pl.pallas_call(functools.partial(gather_kernel, zs), out_shape=[jax.Shape...  117 us
    pallas_call x1, Pallas kernels, attend(): pl.pallas_call(functools.partial(attend_kernel, cblks, heads), out_shape=...  49 us
    pallas_call x1, Pallas kernels, finish(): pl.pallas_call(functools.partial(finish_kernel, zs), out_shape=jax.ShapeD...  28.5 us
    ppermute x3, starting transfers between devices, on_device(): lax.ppermute(pattern[0], 'cache', ring_pairs(-k))  5.74 us
  transfers between devices with their start and end apart: 3, of which 0 were waited for; matrix products, arithmetic and copies ran while one was open for 3% of the time, Pallas kernels for 55%

profile of v2, /device:TPU:0, one launch (start us, length us, event | category | flops | bytes accessed | tf_op | source)
XLA Modules:
  0.0 213.3 jit_solution(10833301825931628714)
XLA Ops:
  0.0 1.6 collective-permute-start.2
  1.6 2.7 %collective-permute-start.1 = (s32[4,64]{1,0:T(4,128)}, s32[4,64]{1,0:T(4,128)S(1)}, u32[]{:S(2)}, u32[]{:S(2)}) collective-permute-start(s32[4,64]{1,0:T(4,128)} %bitcast.40), channel_id=1, source_target_pairs={{0,64},{4,20},{8,72},{12,28},{16,80},{20,4},{24,88},{28,12},{32,96... | collective-permute-start | bytes 3080 | tf_op jit(solution)/shard_map/ppermute | solution.py:483
  4.3 1.4 collective-permute-start
  5.8 0.7 add_select_fusion
  6.5 0.7 broadcast_compare_fusion
  7.4 0.1 fusion.8
  7.5 0.6 gather_fusion.1
  8.0 0.9 convert_reduce_fusion
  8.9 0.6 gather_fusion.2
  9.5 0.1 stack.71
  9.6 0.1 select_reduce_fusion.2
  9.7 0.1 select_reduce_fusion.1
  9.9 0.8 fusion.5
  10.7 0.1 copy.47
  10.8 0.7 reshape.289.send_ref
  11.5 1.0 copy.48.ids_ref
  12.5 0.0 copy-start.5
  12.5 116.7 %gather.19 = (bf16[8,4,4,512,128]{4,3,2,1,0:T(8,128)(2,1)}, bf16[4,1024,256]{2,1,0:T(8,128)(2,1)}, bf16[256,1024]{1,0:T(8,128)(2,1)}, f32[256,1024]{1,0:T(8,128)}) custom-call(s32[128]{0:T(128)} %reshape.289.send_ref, s32[1024,1]{1,0:T(8,128)} %copy.48.ids_ref, bf16[64,512,128]{2,1,0:T(8,128)(2,1)} %bitcast.36, bf16[2048,1024]{1,0:T(8,128)(2,1)} %table_ref.1, ...), custom_call_target="tpu_custom_call" | custom-call | tf_op jit(solution)/shard_map/gather/pallas_call | solution.py:235
  129.3 0.0 collective-permute-done.2
  129.3 0.0 collective-permute-done.1
  129.3 0.0 collective-permute-done
  129.3 0.0 copy-done.5
  129.3 0.6 gather_fusion
  129.9 0.1 convert_reduce_fusion.2
  130.1 0.1 copy.43
  130.2 0.1 reshape.288.count_ref
  130.2 0.4 convert_reduce_fusion.1
  130.6 2.5 %select_reduce_fusion = s32[4,4,36]{1,2,0:T(8,128)S(1)} fusion(s32[4,64]{1,0:T(4,128)S(1)} %broadcast_add_fusion.1, s32[4,4,64]{2,1,0:T(4,128)S(1)} %convert_reduce_fusion.1, pred[4,4,64]{2,1,0:T(4,128)(4,1)S(1)} %copy.44), kind=kLoop, calls=%fused_computation.5 | loop fusion | flops 146880 | bytes 8448 | tf_op jit(solution)/shard_map/reduce_sum | solution.py:496
  133.1 0.1 copy.49
  133.2 0.1 add.326.list_ref
  133.3 0.0 copy-start.4
  133.3 1.6 copy-done.4
  134.9 0.0 copy-start
  134.9 0.0 copy-start.1
  134.9 0.0 copy-start.2
  134.9 0.0 copy-start.3
  134.9 49.0 %attend.1.o_ref = bf16[4,1024,256]{2,1,0:T(8,128)(2,1)S(1)} custom-call(s32[16]{0:T(128)S(1)} %reshape.288.count_ref, s32[576]{0:T(1024)S(1)} %add.326.list_ref, bf16[4,1024,256]{2,1,0:T(8,128)(2,1)S(1)} %copy-done.4, bf16[8,4,4,4,128,128]{5,4,3,2,1,0:T(8,128)(2,1)} %bitcast.46), custom_call_target="tpu_custom_call" | custom-call | flops 68719476736 | bytes 25165824 | tf_op jit(solution)/shard_map/attend/pallas_call | solution.py:332
  183.9 0.0 copy-done
  183.9 0.0 copy-done.1
  183.9 0.0 copy-done.2
  183.9 0.0 copy-done.3
  184.0 28.5 %finish.1 = bf16[256,1024]{1,0:T(8,128)(2,1)S(1)} custom-call(bf16[4,1024,256]{2,1,0:T(8,128)(2,1)S(1)} %attend.1.o_ref, bf16[256,1024]{1,0:T(8,128)(2,1)S(1)} %copy-done.2, f32[256,1024]{1,0:T(8,128)S(1)} %copy-done.1, f32[1,1024]{1,0:T(1,128)S(1)} %bitcast.35, bf16[1024,1024]{1,0:T(8,128)(2,1)S(1)} %copy-done), custom_call_target="tpu_custom_call" | custom-call | tf_op jit(solution)/shard_map/finish/pallas_call | solution.py:423
  212.5 0.8 copy.51
  (10 shorter events, 0.1 us)
Async XLA Ops:
  0.0 129.3 %collective-permute-start.2 = (s32[4,64]{1,0:T(4,128)}, s32[4,64]{1,0:T(4,128)S(1)}, u32[]{:S(2)}, u32[]{:S(2)}) collective-permute-start(s32[4,64]{1,0:T(4,128)} %bitcast.39), channel_id=1, source_target_pairs={{0,32},{4,12},{8,40},{12,20},{16,48},{20,28},{24,56},{28,4},{32,64... | collective-permute-start | bytes 3080 | tf_op jit(solution)/shard_map/ppermute | solution.py:483
  1.6 127.7 %collective-permute-start.1 = (s32[4,64]{1,0:T(4,128)}, s32[4,64]{1,0:T(4,128)S(1)}, u32[]{:S(2)}, u32[]{:S(2)}) collective-permute-start(s32[4,64]{1,0:T(4,128)} %bitcast.40), channel_id=1, source_target_pairs={{0,64},{4,20},{8,72},{12,28},{16,80},{20,4},{24,88},{28,12},{32,96... | collective-permute-start | bytes 3080 | tf_op jit(solution)/shard_map/ppermute | solution.py:483
  4.3 125.0 %collective-permute-start = (s32[4,64]{1,0:T(4,128)}, s32[4,64]{1,0:T(4,128)S(1)}, u32[]{:S(2)}, u32[]{:S(2)}) collective-permute-start(s32[4,64]{1,0:T(4,128)} %bitcast.41), channel_id=1, source_target_pairs={{0,96},{4,28},{8,104},{12,4},{16,112},{20,12},{24,120},{28,20},{32... | collective-permute-start | bytes 3080 | tf_op jit(solution)/shard_map/ppermute | solution.py:483
  12.5 116.8 %copy-start.5 = (s32[1,4,64]{2,1,0:T(4,128)S(1)}, s32[1,4,64]{2,1,0:T(4,128)}, u32[]{:S(2)}) copy-start(s32[1,4,64]{2,1,0:T(4,128)} %param.13) | copy-start | bytes 3076
  133.3 1.6 copy-start.4
  134.9 49.0 %copy-start = (bf16[1024,1024]{1,0:T(8,128)(2,1)S(1)}, bf16[1024,1024]{1,0:T(8,128)(2,1)}, u32[]{:S(2)}) copy-start(bf16[1024,1024]{1,0:T(8,128)(2,1)} %w_ref.1) | copy-start | bytes 6291460
  134.9 49.0 %copy-start.1 = (f32[256,1024]{1,0:T(8,128)S(1)}, f32[256,1024]{1,0:T(8,128)}, u32[]{:S(2)}) copy-start(f32[256,1024]{1,0:T(8,128)} %get-tuple-element.12.gate_ref) | copy-start | bytes 3145732
  134.9 49.0 %copy-start.2 = (bf16[256,1024]{1,0:T(8,128)(2,1)S(1)}, bf16[256,1024]{1,0:T(8,128)(2,1)}, u32[]{:S(2)}) copy-start(bf16[256,1024]{1,0:T(8,128)(2,1)} %get-tuple-element.11.embedded_ref) | copy-start | bytes 1572868
  134.9 49.0 %copy-start.3 = (f32[1024]{0:T(1024)S(1)}, f32[1024]{0:T(1024)}, u32[]{:S(2)}) copy-start(f32[1024]{0:T(1024)} %param.16) | copy-start | bytes 12292

commit v3 on v2

v3 whole, which is shorter than its diff:
```python
import functools
import jax
import jax.numpy as jnp
from jax import lax
from jax.experimental import pallas as pl
from jax.experimental.pallas import tpu as pltpu
from jax.sharding import PartitionSpec as P

DH = 64
BLK = 128
SLOT = 4
CB = 256
RING = 4
SOURCES = 8
STEP = 256
HOPS = (2, 1, 3)
ORDER = (0, 2, 1, 3)

norm_eps = 1e-05
MESH = pl.DeviceIdType.MESH


def at(x, y, core):
    return (lax.rem(x + 2 * RING, RING) * RING + lax.rem(y + 2 * RING, RING)) * 2 + core


def place():
    me = lax.axis_index("cache")
    core = lax.rem(me, 2)
    y = lax.rem(lax.div(me, 2), RING)
    x = lax.div(me, 2 * RING)
    return x, y, core


def ring_peer(k):
    x, y, core = place()
    return jnp.where(core == 0, at(x + k, y, 0), at(x, y + k, 1))


def kv_dest(i):
    x, y, core = place()
    j, s = lax.div(i, 2), lax.rem(i, 2)
    return jnp.where(core == s, at(x, y + j, 0), at(x + j, y, 1))


def kv_source(i):
    x, y, core = place()
    j, s = lax.div(i, 2), lax.rem(i, 2)
    return jnp.where(core == 0, at(x, y - j, s), at(x - j, y, 1 - s))


def kv_request(i, k):
    x, y, core = place()
    j, s = lax.div(i, 2), lax.rem(i, 2)
    return jnp.where(core == s, at(x + k, y + j, 0), at(x + j, y + k, 1))


def ring_pairs(k):
    pairs = []
    for x in range(RING):
        for y in range(RING):
            here = (x * RING + y) * 2
            pairs.append((here, ((x + k) % RING * RING + y) * 2))
            pairs.append((here + 1, (x * RING + (y + k) % RING) * 2 + 1))
    return pairs


def layer_kernel(
    zs, send_ref, mask_ref, ids_ref, kv_ref, table_ref, wq_ref, wg_ref, gain_ref, wo_ref,
    recv_ref, out_ref,
    stage, turn, parts, parts_in, chunks, queries, gate, held, keys, acc, own, sums, sums_in, pieces, pieces_in,
    kv_out, kv_in, z1_out, z1_in, z2_out, z2_in, q_out, q_in, held_sem, o_out, o_in, z3_out, z3_in,
):
    z = lax.axis_index("item")
    rows, width = out_ref.shape
    part = width // zs
    heads = part // DH
    peer_z = lambda d: lax.rem(z + d + zs, zs)

    barrier = pltpu.get_barrier_semaphore()
    for i in range(1, SOURCES):
        pl.semaphore_signal(barrier, inc=1, device_id={"cache": kv_source(i)}, device_id_type=MESH)
    for k in HOPS:
        pl.semaphore_signal(barrier, inc=1, device_id={"cache": ring_peer(k)}, device_id_type=MESH)
        pl.semaphore_signal(barrier, inc=1, device_id={"item": peer_z(k)}, device_id_type=MESH)
    pl.semaphore_wait(barrier, SOURCES - 1 + 2 * len(HOPS))

    to = lax.broadcasted_iota(jnp.int32, turn.shape, 0)
    of = lax.broadcasted_iota(jnp.int32, turn.shape, 1)
    turn[...] = jnp.where(
        of == lax.rem(to, BLK) * heads + lax.div(to, BLK), 1.0, 0.0
    ).astype(turn.dtype)

    def kv_copy(i, k):
        return pltpu.make_async_remote_copy(
            src_ref=stage.at[i, k],
            dst_ref=recv_ref.at[i, k],
            send_sem=kv_out.at[i * RING + k],
            recv_sem=kv_in.at[i * RING + k],
            device_id={"cache": kv_dest(i)},
            device_id_type=MESH,
        )

    def own_copy(k):
        return pltpu.make_async_copy(stage.at[0, k], recv_ref.at[0, k], kv_out.at[k])

    def send_blocks(k):
        def step(n, carry):
            i = lax.rem(n + 2, SOURCES)
            request = kv_request(i, k)
            for slot in range(SLOT):
                block = kv_ref[send_ref[request * SLOT + slot]]
                by_head = jnp.dot(turn[...], block, preferred_element_type=jnp.float32)
                turned = by_head.T.astype(stage.dtype)
                by_head = by_head.astype(stage.dtype)
                for p in range(heads // 2):
                    stage[i, k, slot, p * BLK : (p + 1) * BLK, :] = jnp.concatenate(
                        [by_head[h * BLK : (h + 1) * BLK, :DH] for h in (2 * p, 2 * p + 1)], axis=1
                    )
                for h in range(heads):
                    first = heads // 2 * BLK + h * DH
                    stage[i, k, slot, first : first + DH, :] = turned[DH:, h * BLK : (h + 1) * BLK]

            @pl.when(i == 0)
            def _():
                own_copy(k).start()

            @pl.when(i != 0)
            def _():
                kv_copy(i, k).start()

            return carry

        lax.fori_loop(0, SOURCES, step, 0)

    def z1_copy(d):
        return pltpu.make_async_remote_copy(
            src_ref=parts.at[d],
            dst_ref=parts_in.at[d - 1],
            send_sem=z1_out.at[d - 1],
            recv_sem=z1_in.at[d - 1],
            device_id={"item": peer_z(d)},
            device_id_type=MESH,
        )

    def z2_copy(d):
        return pltpu.make_async_remote_copy(
            src_ref=chunks.at[0],
            dst_ref=chunks.at[d],
            send_sem=z2_out.at[d - 1],
            recv_sem=z2_in.at[d - 1],
            device_id={"item": peer_z(d)},
            device_id_type=MESH,
        )

    def q_copy(k):
        return pltpu.make_async_remote_copy(
            src_ref=queries.at[0],
            dst_ref=queries.at[k],
            send_sem=q_out.at[k - 1],
            recv_sem=q_in.at[k - 1],
            device_id={"cache": ring_peer(-k)},
            device_id_type=MESH,
        )

    def o_copy(k):
        return pltpu.make_async_remote_copy(
            src_ref=sums.at[k - 1],
            dst_ref=sums_in.at[k - 1],
            send_sem=o_out.at[k - 1],
            recv_sem=o_in.at[k - 1],
            device_id={"cache": ring_peer(k)},
            device_id_type=MESH,
        )

    def z3_copy(i):
        return pltpu.make_async_remote_copy(
            src_ref=pieces.at[i],
            dst_ref=pieces_in.at[i - 1],
            send_sem=z3_out.at[i - 1],
            recv_sem=z3_in.at[i - 1],
            device_id={"item": peer_z(-i)},
            device_id_type=MESH,
        )

    send_blocks(ORDER[0])

    for d in HOPS + (0,):
        ids = ids_ref[d * rows : (d + 1) * rows, :]
        hot = ids == lax.broadcasted_iota(jnp.int32, (rows, table_ref.shape[0]), 1)
        parts[d] = jnp.dot(
            jnp.where(hot, 1.0, 0.0).astype(table_ref.dtype),
            table_ref[...],
            preferred_element_type=jnp.float32,
        ).astype(parts.dtype)
        if d != 0:
            z1_copy(d).start()

    send_blocks(ORDER[1])

    for d in HOPS:
        z1_copy(d).wait_recv()
    chunks[0] = parts[0] + parts_in[0] + parts_in[1] + parts_in[2]
    for d in HOPS:
        z2_copy(d).start()

    send_blocks(ORDER[2])
    send_blocks(ORDER[3])

    def silu(v):
        return v * jax.nn.sigmoid(v)

    gate[...] = silu(jnp.dot(chunks[0], wg_ref[...], preferred_element_type=jnp.float32))
    scale = 0.5 * DH ** (-0.5)
    for d in (0,) + HOPS:
        if d != 0:
            z2_copy(d).wait_recv()
        queries[0, :, d * rows : (d + 1) * rows] = silu(
            lax.dot_general(
                wq_ref[...], chunks[d], (((1,), (1,)), ((), ())), preferred_element_type=jnp.float32
            )
        ).astype(queries.dtype) * jnp.asarray(scale, queries.dtype)
    for k in HOPS:
        q_copy(k).start()

    def unit(u):
        place_in = lax.div(u, SOURCES)
        k = jnp.int32(ORDER[0])
        for p in range(1, RING):
            k = jnp.where(place_in == p, ORDER[p], k)
        return lax.rem(lax.rem(u, SOURCES) + 2, SOURCES), k

    def fetch(u):
        i, k = unit(u)
        return pltpu.make_async_copy(recv_ref.at[i, k], held.at[lax.rem(u, 2)], held_sem.at[lax.rem(u, 2)])

    def start_fetch(u):
        i, k = unit(u)

        @pl.when(i == 0)
        def _():
            own_copy(k).wait()

        @pl.when(i != 0)
        def _():
            kv_copy(i, k).wait_recv()

        fetch(u).start()

    units = SOURCES * RING
    start_fetch(0)
    fetch(0).wait()

    def one_unit(u, carry):
        i, k = unit(u)
        n = lax.rem(u, SOURCES)
        buf = lax.rem(u, 2)

        @pl.when(u + 1 < units)
        def _():
            start_fetch(u + 1)

        @pl.when(n == 0)
        def _():
            acc[...] = jnp.zeros_like(acc)

            @pl.when(k != 0)
            def _():
                q_copy(k).wait_recv()

        for slot in range(SLOT):
            at_slot = slice(slot * BLK, (slot + 1) * BLK)
            for p in range(heads // 2):
                pair = held[buf, slot, p * BLK : (p + 1) * BLK, :]
                keys[2 * p, at_slot, :] = pair[:, :DH]
                keys[2 * p + 1, at_slot, :] = pair[:, DH:]
        wanted = [
            [mask_ref[((k * SOURCES + i) * zs + b) * SLOT + slot].astype(keys.dtype) for slot in range(SLOT)]
            for b in range(zs)
        ]

        def half_scores(h, t):
            return jnp.dot(
                keys[h, t * STEP : (t + 1) * STEP, :],
                queries[k, h * DH : (h + 1) * DH, :],
                preferred_element_type=jnp.float32,
            )

        def add_values(h, t, weights):
            first = heads // 2 * BLK + h * DH
            slots = range(t * STEP // BLK, (t + 1) * STEP // BLK)
            values = [held[buf, slot, first : first + DH, :] for slot in slots]
            for b in range(zs):
                cols = slice(b * rows, (b + 1) * rows)
                masked = jnp.concatenate([v * wanted[b][s] for s, v in zip(slots, values)], axis=1)
                acc[h * DH : (h + 1) * DH, cols] += jnp.dot(
                    masked, weights[:, cols], preferred_element_type=jnp.float32
                )

        steps = [(h, t) for h in range(heads) for t in range(SLOT * BLK // STEP)]
        scores = half_scores(*steps[0])
        for m, (h, t) in enumerate(steps):
            later = half_scores(*steps[m + 1]) if m + 1 < len(steps) else None
            add_values(h, t, (scores + scores * jnp.tanh(scores)).astype(keys.dtype))
            scores = later

        @pl.when((n == SOURCES - 1) & (k == 0))
        def _():
            own[...] = acc[...]

        @pl.when((n == SOURCES - 1) & (k != 0))
        def _():
            sums[k - 1] = acc[...].astype(sums.dtype)
            o_copy(k).start()

        @pl.when(u + 1 < units)
        def _():
            fetch(u + 1).wait()

        return carry

    lax.fori_loop(0, units, one_unit, 0)

    for k in ORDER[1:]:
        o_copy(k).wait_recv()
        if k != ORDER[3]:
            own[...] += sums_in[k - 1].astype(jnp.float32)
    mine = None
    for i in HOPS + (0,):
        cols = slice(i * rows, (i + 1) * rows)
        total = (own[:, cols] + sums_in[ORDER[3] - 1, :, cols].astype(jnp.float32)).T
        if i == 0:
            mine = total
        else:
            pieces[i] = total.astype(pieces.dtype)
            z3_copy(i).start()
    for i in HOPS:
        z3_copy(i).wait_recv()
    attended = [mine] + [pieces_in[i - 1].astype(jnp.float32) for i in range(1, zs)]
    row_mean = sum(jnp.sum(a, axis=1, keepdims=True) for a in attended) / width
    row_square = sum(jnp.sum(a * a, axis=1, keepdims=True) for a in attended) / width
    norm = lax.rsqrt(row_square - row_mean * row_mean + norm_eps)
    total = chunks[0].astype(jnp.float32)
    for i, a in enumerate(attended):
        cols = pl.ds(pl.multiple_of(peer_z(i) * part, part), part)
        hidden = (a - row_mean) * norm * gain_ref[:, cols] * gate[:, cols]
        total += jnp.dot(
            hidden.astype(jnp.bfloat16), wo_ref[cols, :], preferred_element_type=jnp.float32
        )
    out_ref[...] = total.astype(out_ref.dtype)

    for d in HOPS:
        z1_copy(d).wait_send()
        z2_copy(d).wait_send()
        z3_copy(d).wait_send()
        q_copy(d).wait_send()
        o_copy(d).wait_send()

    def drain(n, carry):
        kv_copy(lax.div(n, RING) + 1, lax.rem(n, RING)).wait_send()
        return carry

    lax.fori_loop(0, (SOURCES - 1) * RING, drain, 0)


def layer(zs, send, mask, ids, kv, table, w_query, w_gate, norm_gain, w_out):
    smem = pl.BlockSpec(memory_space=pltpu.SMEM)
    vmem = pl.BlockSpec(memory_space=pltpu.VMEM)
    hbm = pl.BlockSpec(memory_space=pl.ANY)
    cands = ids.shape[0]
    rows = cands // zs
    width = table.shape[1]
    part = w_query.shape[0]
    heads = part // DH
    kind = kv.dtype
    dma = pltpu.SemaphoreType.DMA
    moved = (SOURCES, RING, SLOT) + kv.shape[1:]
    return pl.pallas_call(
        functools.partial(layer_kernel, zs),
        out_shape=[jax.ShapeDtypeStruct(moved, kind), jax.ShapeDtypeStruct((rows, width), kind)],
        in_specs=[smem, smem] + [vmem] * 7,
        out_specs=[hbm, vmem],
        scratch_shapes=[
            pltpu.VMEM(moved, kind),
            pltpu.VMEM((kv.shape[1], kv.shape[1]), kind),
            pltpu.VMEM((zs, rows, width), kind),
            pltpu.VMEM((zs - 1, rows, width), kind),
            pltpu.VMEM((zs, rows, width), kind),
            pltpu.VMEM((RING, part, cands), kind),
            pltpu.VMEM((rows, width), jnp.float32),
            pltpu.VMEM((2, SLOT) + kv.shape[1:], kind),
            pltpu.VMEM((heads, SLOT * BLK, DH), kind),
            pltpu.VMEM((part, cands), jnp.float32),
            pltpu.VMEM((part, cands), jnp.float32),
            pltpu.VMEM((RING - 1, part, cands), kind),
            pltpu.VMEM((RING - 1, part, cands), kind),
            pltpu.VMEM((zs, rows, part), kind),
            pltpu.VMEM((zs - 1, rows, part), kind),
            dma((SOURCES * RING,)),
            dma((SOURCES * RING,)),
            dma((zs - 1,)),
            dma((zs - 1,)),
            dma((zs - 1,)),
            dma((zs - 1,)),
            dma((RING - 1,)),
            dma((RING - 1,)),
            dma((2,)),
            dma((RING - 1,)),
            dma((RING - 1,)),
            dma((zs - 1,)),
            dma((zs - 1,)),
        ],
        compiler_params=pltpu.CompilerParams(
            collective_id=0, has_side_effects=True, vmem_limit_bytes=60 * 2**20
        ),
        name="layer",
    )(send, mask, ids, kv, table, w_query, w_gate, norm_gain, w_out)[1]


def on_device(
    cand_items, item_table, kv_cache, hist_blocks, pattern, w_query, w_gate, norm_gain, w_out
):
    zs = lax.axis_size("item")
    z = lax.axis_index("item")
    me = lax.axis_index("cache")
    blocks_here = kv_cache.shape[0]
    list_len = hist_blocks.shape[1]
    item_ids = cand_items[0]
    rows_per = item_ids.shape[0] // zs

    owner_of = hist_blocks // blocks_here
    local_of = hist_blocks % blocks_here
    same_owner = owner_of[:, :, None] == owner_of[:, None, :]
    positions = jnp.arange(list_len)
    earlier = positions[None, :] < positions[:, None]
    slot_rank = jnp.sum(same_owner & earlier[None], axis=2)
    slots = jnp.arange(SLOT)
    selected = (owner_of == me)[:, None, :] & (slot_rank[:, None, :] == slots[None, :, None])
    send = jnp.sum(jnp.where(selected, local_of[:, None, :], 0), axis=2)

    turned = lax.dynamic_slice_in_dim(
        jnp.concatenate([item_ids, item_ids]), z * rows_per, item_ids.shape[0], 0
    )
    local_ids = (turned - z * item_table.shape[0])[:, None]
    kv_rows = kv_cache.reshape(blocks_here, -1, kv_cache.shape[3])

    request = jnp.stack([ring_peer(k) for k in range(RING)])
    owner_idx = jnp.stack([kv_source(i) for i in range(SOURCES)])
    rotation = (z - jnp.arange(zs)) % zs
    pattern_of = [pattern[0]] + [
        lax.ppermute(pattern[0], "cache", ring_pairs(-k)) for k in range(1, RING)
    ]
    pattern_k = jnp.stack(pattern_of)[:, rotation]
    from_source = owner_of[request][:, None, None, :] == owner_idx[None, :, None, None]
    in_slot = slot_rank[request][:, None, None, :] == slots[None, None, :, None]
    filled = from_source & in_slot
    mask = jnp.any(filled[:, :, None] & (pattern_k != 0)[:, None, :, None], axis=4)
    out = layer(
        zs,
        send.reshape(-1).astype(jnp.int32),
        mask.reshape(-1).astype(jnp.float32),
        local_ids,
        kv_rows,
        item_table,
        w_query.T,
        w_gate,
        norm_gain[None, :],
        w_out,
    )
    return out[None]


def solution(mesh):
    placed = (
        P("cache", None),
        P("item", None),
        P("cache", None, "item", None),
        P(),
        P("cache", None, None),
        P(None, "item"),
        P(),
        P(),
        P(),
    )
    return jax.shard_map(
        on_device, mesh=mesh, in_specs=placed, out_specs=P("cache", "item", None), check_vma=False
    )
```

time: 217 us -> 202 us (0.931)
  Pallas kernels: 194 us -> 181 us
    pallas_call x3 -> x1, Pallas kernels: 194 us -> 181 us  [layer(): pl.pallas_call(functools.partial(layer_kernel, zs), out_shape=[jax.ShapeD...]
    reduce_sum x4 -> x0, other arithmetic: 3.11 us -> none  [the longest x1 2.5 us: on_device(): jnp.sum(jnp.where(wanted[:, :, None, :] & (before[:, :, None, :] == place...]
  transfers between devices with their start and end apart: 3 -> 3, of which waited for: 0 -> 0; matrix products, arithmetic and copies ran while one was open for 3% -> 4% of each run, Pallas kernels for 55% -> 0%
where the time goes in v3:
time: 202 us; the launch traced here: 200 us
  Pallas kernels  181 us (90%)
  local copies, waits for them, and re-layouts  8.4 us (4%)
  starting transfers between devices  5.74 us (3%)
  other arithmetic  5.51 us (3%)
    pallas_call x1, Pallas kernels, layer(): pl.pallas_call(functools.partial(layer_kernel, zs), out_shape=[jax.ShapeD...  181 us
    ppermute x3, starting transfers between devices, on_device(): lax.ppermute(pattern[0], 'cache', ring_pairs(-k))  5.74 us
  transfers between devices with their start and end apart: 3, of which 0 were waited for; matrix products, arithmetic and copies ran while one was open for 4% of the time, Pallas kernels for 0%

profile of v3, /device:TPU:0, one launch (start us, length us, event | category | flops | bytes accessed | tf_op | source)
XLA Modules:
  0.0 200.4 jit_solution(2424269311179287302)
XLA Ops:
  0.0 1.6 collective-permute-start.2
  1.6 2.7 %collective-permute-start.1 = (s32[4,64]{1,0:T(4,128)}, s32[4,64]{1,0:T(4,128)S(1)}, u32[]{:S(2)}, u32[]{:S(2)}) collective-permute-start(s32[4,64]{1,0:T(4,128)} %bitcast.40), channel_id=1, source_target_pairs={{0,64},{4,20},{8,72},{12,28},{16,80},{20,4},{24,88},{28,12},{32,96... | collective-permute-start | bytes 3080 | tf_op jit(solution)/shard_map/ppermute | solution.py:451
  4.3 1.4 collective-permute-start
  5.8 0.7 add_select_fusion
  6.5 0.7 broadcast_compare_fusion.1
  7.4 0.1 fusion.6
  7.5 0.6 gather_fusion
  8.0 0.9 convert_reduce_fusion
  8.9 0.6 gather_fusion.1
  9.5 0.1 select_reduce_fusion
  9.7 0.1 stack.67
  9.8 0.1 broadcast_compare_fusion
  9.9 0.8 fusion.4
  10.7 0.1 copy.17
  10.8 0.7 reshape.256.send_ref
  11.5 1.0 copy.24.ids_ref
  12.5 2.0 %copy.23 = bf16[1024,256]{0,1:T(8,128)(2,1)} copy(bf16[1024,256]{1,0:T(8,128)(2,1)} %param.14) | data formatting | bytes 1048576 | tf_op args[5]
  14.6 0.0 collective-permute-done.2
  14.6 0.0 collective-permute-done.1
  14.6 0.0 collective-permute-done
  14.6 0.7 pad_add_fusion
  15.3 0.6 gather_fusion.2
  15.9 1.2 and_reduce_fusion
  17.1 0.2 copy.22
  17.2 0.7 reshape.258.mask_ref
  18.0 180.5 %layer.1 = (bf16[8,4,4,512,128]{4,3,2,1,0:T(8,128)(2,1)}, bf16[256,1024]{1,0:T(8,128)(2,1)}) custom-call(s32[128]{0:T(128)} %reshape.256.send_ref, f32[512]{0:T(512)} %reshape.258.mask_ref, s32[1024,1]{1,0:T(8,128)} %copy.24.ids_ref, bf16[64,512,128]{2,1,0:T(8,128)(2,1)} %bitcast.33, bf16[2048,1024]{1,0:T(8,128)(2,1)} %table_ref.1, ...), custom_call_target="tpu_custom_call" | custom-call | tf_op jit(solution)/shard_map/layer/pallas_call | solution.py:378
  198.5 1.9 copy.26
  (9 shorter events, 0.1 us)
Async XLA Ops:
  0.0 14.6 %collective-permute-start.2 = (s32[4,64]{1,0:T(4,128)}, s32[4,64]{1,0:T(4,128)S(1)}, u32[]{:S(2)}, u32[]{:S(2)}) collective-permute-start(s32[4,64]{1,0:T(4,128)} %bitcast.39), channel_id=1, source_target_pairs={{0,32},{4,12},{8,40},{12,20},{16,48},{20,28},{24,56},{28,4},{32,64... | collective-permute-start | bytes 3080 | tf_op jit(solution)/shard_map/ppermute | solution.py:451
  1.6 13.0 %collective-permute-start.1 = (s32[4,64]{1,0:T(4,128)}, s32[4,64]{1,0:T(4,128)S(1)}, u32[]{:S(2)}, u32[]{:S(2)}) collective-permute-start(s32[4,64]{1,0:T(4,128)} %bitcast.40), channel_id=1, source_target_pairs={{0,64},{4,20},{8,72},{12,28},{16,80},{20,4},{24,88},{28,12},{32,96... | collective-permute-start | bytes 3080 | tf_op jit(solution)/shard_map/ppermute | solution.py:451
  4.3 10.3 %collective-permute-start = (s32[4,64]{1,0:T(4,128)}, s32[4,64]{1,0:T(4,128)S(1)}, u32[]{:S(2)}, u32[]{:S(2)}) collective-permute-start(s32[4,64]{1,0:T(4,128)} %bitcast.41), channel_id=1, source_target_pairs={{0,96},{4,28},{8,104},{12,4},{16,112},{20,12},{24,120},{28,20},{32... | collective-permute-start | bytes 3080 | tf_op jit(solution)/shard_map/ppermute | solution.py:451

commit v4 on v3

--- a/solution.py
+++ b/solution.py
@@ -55,27 +55,34 @@
     return jnp.where(core == s, at(x + k, y + j, 0), at(x + j, y + k, 1))
 
 
-def ring_pairs(k):
-    pairs = []
-    for x in range(RING):
-        for y in range(RING):
-            here = (x * RING + y) * 2
-            pairs.append((here, ((x + k) % RING * RING + y) * 2))
-            pairs.append((here + 1, (x * RING + (y + k) % RING) * 2 + 1))
-    return pairs
+def source_at(n):
+    return jnp.where(n < 2, n + 2, jnp.where(n < 4, n + 4, jnp.where(n < 6, 5 - n, n - 2)))
 
 
 def layer_kernel(
-    zs, send_ref, mask_ref, ids_ref, kv_ref, table_ref, wq_ref, wg_ref, gain_ref, wo_ref,
+    zs, send_ref, where_ref, ids_ref, pattern_ref, gain_ref, kv_hbm, table_hbm, wq_hbm, wg_hbm, wo_hbm,
     recv_ref, out_ref,
-    stage, turn, parts, parts_in, chunks, queries, gate, held, keys, acc, own, sums, sums_in, pieces, pieces_in,
-    kv_out, kv_in, z1_out, z1_in, z2_out, z2_in, q_out, q_in, held_sem, o_out, o_in, z3_out, z3_in,
+    kv_ref, table_ref, wq_ref, wg_ref, wo_ref, wq_turned, pattern_in, patterns,
+    stage, turn, parts, relay_in, parts_in, chunks, queries, gate, held, keys, acc, own, sums, sums_in,
+    pieces, pieces_in,
+    load_sem, pat_out, pat_in, pat_here, kv_out, kv_in, z1_out, z1_in, z2_out, z2_in, q_out, q_in, held_sem,
+    o_out, o_in, z3_out, z3_in,
 ):
     z = lax.axis_index("item")
     rows, width = out_ref.shape
     part = width // zs
     heads = part // DH
+    half = rows // 2
     peer_z = lambda d: lax.rem(z + d + zs, zs)
+
+    loads = [
+        pltpu.make_async_copy(src, dst, load_sem.at[n])
+        for n, (src, dst) in enumerate(
+            [(table_hbm, table_ref), (kv_hbm, kv_ref), (wq_hbm, wq_ref), (wg_hbm, wg_ref), (wo_hbm, wo_ref)]
+        )
+    ]
+    for load in loads:
+        load.start()
 
     barrier = pltpu.get_barrier_semaphore()
     for i in range(1, SOURCES):
@@ -104,9 +111,9 @@
     def own_copy(k):
         return pltpu.make_async_copy(stage.at[0, k], recv_ref.at[0, k], kv_out.at[k])
 
-    def send_blocks(k):
+    def send_blocks(k, first, last):
         def step(n, carry):
-            i = lax.rem(n + 2, SOURCES)
+            i = source_at(n)
             request = kv_request(i, k)
             for slot in range(SLOT):
                 block = kv_ref[send_ref[request * SLOT + slot]]
@@ -131,27 +138,54 @@
 
             return carry
 
-        lax.fori_loop(0, SOURCES, step, 0)
-
-    def z1_copy(d):
+        lax.fori_loop(first, last, step, 0)
+
+    halves = {1: pl.ds(0, half), -1: pl.ds(half, half)}
+
+    def z_remote(src, dst, out_sem, in_sem, d):
         return pltpu.make_async_remote_copy(
-            src_ref=parts.at[d],
-            dst_ref=parts_in.at[d - 1],
-            send_sem=z1_out.at[d - 1],
-            recv_sem=z1_in.at[d - 1],
-            device_id={"item": peer_z(d)},
+            src_ref=src, dst_ref=dst, send_sem=out_sem, recv_sem=in_sem,
+            device_id={"item": peer_z(d)}, device_id_type=MESH,
+        )
+
+    def relay_copy(way):
+        n = 0 if way == 1 else 1
+        return z_remote(
+            parts.at[2, halves[way]], relay_in.at[n], z1_out.at[n], z1_in.at[n], way
+        )
+
+    def part_copy(way, h):
+        n = 0 if way == 1 else 1
+        sem = 2 + 2 * n + (0 if h == 1 else 1)
+        return z_remote(
+            parts.at[way % zs, halves[h]], parts_in.at[n, halves[h]], z1_out.at[sem], z1_in.at[sem], way
+        )
+
+    def chunk_copy(way, h):
+        n = (0 if way == 1 else 2) + (0 if h == 1 else 1)
+        return z_remote(
+            chunks.at[0, halves[h]], chunks.at[way % zs, halves[h]], z2_out.at[n], z2_in.at[n], way
+        )
+
+    def pass_copy(way):
+        n = 4 if way == 1 else 5
+        return z_remote(
+            chunks.at[way % zs, halves[way]], chunks.at[2, halves[way]], z2_out.at[n], z2_in.at[n], way
+        )
+
+    def pattern_copy(k):
+        return pltpu.make_async_remote_copy(
+            src_ref=pattern_ref,
+            dst_ref=pattern_in.at[k - 1],
+            send_sem=pat_out.at[k - 1],
+            recv_sem=pat_in.at[k - 1],
+            device_id={"cache": ring_peer(-k)},
             device_id_type=MESH,
         )
 
-    def z2_copy(d):
-        return pltpu.make_async_remote_copy(
-            src_ref=chunks.at[0],
-            dst_ref=chunks.at[d],
-            send_sem=z2_out.at[d - 1],
-            recv_sem=z2_in.at[d - 1],
-            device_id={"item": peer_z(d)},
-            device_id_type=MESH,
-        )
+    def pattern_here(k):
+        src = pattern_ref if k == 0 else pattern_in.at[k - 1]
+        return pltpu.make_async_copy(src, patterns.at[k], pat_here.at[k])
 
     def q_copy(k):
         return pltpu.make_async_remote_copy(
@@ -183,52 +217,95 @@
             device_id_type=MESH,
         )
 
-    send_blocks(ORDER[0])
-
-    for d in HOPS + (0,):
-        ids = ids_ref[d * rows : (d + 1) * rows, :]
+    for k in HOPS:
+        pattern_copy(k).start()
+    pattern_here(0).start()
+
+    def pick(d):
+        block = peer_z(d)
+        ids = ids_ref[:, pl.ds(pl.multiple_of(block * rows, rows), rows)] - z * table_ref.shape[0]
+        ids = jnp.broadcast_to(ids, (8, rows)).T[:, :1]
         hot = ids == lax.broadcasted_iota(jnp.int32, (rows, table_ref.shape[0]), 1)
         parts[d] = jnp.dot(
             jnp.where(hot, 1.0, 0.0).astype(table_ref.dtype),
             table_ref[...],
             preferred_element_type=jnp.float32,
         ).astype(parts.dtype)
-        if d != 0:
-            z1_copy(d).start()
-
-    send_blocks(ORDER[1])
-
-    for d in HOPS:
-        z1_copy(d).wait_recv()
-    chunks[0] = parts[0] + parts_in[0] + parts_in[1] + parts_in[2]
-    for d in HOPS:
-        z2_copy(d).start()
-
-    send_blocks(ORDER[2])
-    send_blocks(ORDER[3])
+
+    loads[0].wait()
+    pick(2)
+    relay_copy(1).start()
+    relay_copy(-1).start()
+    pick(1)
+    part_copy(1, -1).start()
+    pick(3)
+    part_copy(-1, 1).start()
+    loads[1].wait()
+    send_blocks(0, 0, SOURCES // 2)
+    relay_copy(1).wait()
+    parts[1, halves[1]] += relay_in[0]
+    part_copy(1, 1).start()
+    relay_copy(-1).wait()
+    parts[3, halves[-1]] += relay_in[1]
+    part_copy(-1, -1).start()
+    pick(0)
+    send_blocks(2, 0, SOURCES)
+    for way in (1, -1):
+        for h in (1, -1):
+            part_copy(way, h).wait()
+    chunks[0] = parts[0] + parts_in[0] + parts_in[1]
+    for way in (1, -1):
+        chunk_copy(way, way).start()
+    for way in (1, -1):
+        chunk_copy(way, -way).start()
 
     def silu(v):
         return v * jax.nn.sigmoid(v)
 
-    gate[...] = silu(jnp.dot(chunks[0], wg_ref[...], preferred_element_type=jnp.float32))
+    for load in loads[2:]:
+        load.wait()
+    wq_turned[...] = wq_ref[...].astype(jnp.float32).T.astype(wq_turned.dtype)
     scale = 0.5 * DH ** (-0.5)
-    for d in (0,) + HOPS:
-        if d != 0:
-            z2_copy(d).wait_recv()
+
+    def make_queries(d):
         queries[0, :, d * rows : (d + 1) * rows] = silu(
             lax.dot_general(
-                wq_ref[...], chunks[d], (((1,), (1,)), ((), ())), preferred_element_type=jnp.float32
+                wq_turned[...], chunks[d], (((1,), (1,)), ((), ())), preferred_element_type=jnp.float32
             )
         ).astype(queries.dtype) * jnp.asarray(scale, queries.dtype)
+
+    make_queries(0)
+    for way in (1, -1):
+        chunk_copy(way, way).wait()
+        pass_copy(way).start()
+    send_blocks(1, 0, SOURCES)
+    for way in (1, -1):
+        chunk_copy(way, -way).wait()
+    make_queries(1)
+    make_queries(3)
+    for way in (1, -1):
+        pass_copy(way).wait()
+    make_queries(2)
     for k in HOPS:
         q_copy(k).start()
+    send_blocks(3, 0, SOURCES)
+    send_blocks(0, SOURCES // 2, SOURCES)
+    gate[...] = silu(jnp.dot(chunks[0], wg_ref[...], preferred_element_type=jnp.float32))
+    for k in HOPS:
+        pattern_copy(k).wait()
+        pattern_here(k).start()
+    for k in range(RING):
+        pattern_here(k).wait()
+
+    lead = SOURCES // 2
 
     def unit(u):
-        place_in = lax.div(u, SOURCES)
-        k = jnp.int32(ORDER[0])
-        for p in range(1, RING):
-            k = jnp.where(place_in == p, ORDER[p], k)
-        return lax.rem(lax.rem(u, SOURCES) + 2, SOURCES), k
+        group = lax.div(u + SOURCES - lead, SOURCES)
+        k = jnp.where(group == 1, ORDER[1], jnp.where(group == 2, ORDER[2], ORDER[3]))
+        k = jnp.where((group == 0) | (group == RING), 0, k)
+        n = lax.rem(u + SOURCES - lead, SOURCES)
+        n = jnp.where(group == 0, u, jnp.where(group == RING, u - (RING - 1) * SOURCES, n))
+        return source_at(n), k
 
     def fetch(u):
         i, k = unit(u)
@@ -248,19 +325,22 @@
         fetch(u).start()
 
     units = SOURCES * RING
+    own[...] = jnp.zeros_like(own)
     start_fetch(0)
     fetch(0).wait()
 
     def one_unit(u, carry):
         i, k = unit(u)
-        n = lax.rem(u, SOURCES)
+        n = lax.rem(u + SOURCES - lead, SOURCES)
+        starts = (n == 0) | (u == 0)
+        ends = (n == SOURCES - 1) | (u == units - 1)
         buf = lax.rem(u, 2)
 
         @pl.when(u + 1 < units)
         def _():
             start_fetch(u + 1)
 
-        @pl.when(n == 0)
+        @pl.when(starts)
         def _():
             acc[...] = jnp.zeros_like(acc)
 
@@ -274,10 +354,14 @@
                 pair = held[buf, slot, p * BLK : (p + 1) * BLK, :]
                 keys[2 * p, at_slot, :] = pair[:, :DH]
                 keys[2 * p + 1, at_slot, :] = pair[:, DH:]
-        wanted = [
-            [mask_ref[((k * SOURCES + i) * zs + b) * SLOT + slot].astype(keys.dtype) for slot in range(SLOT)]
-            for b in range(zs)
-        ]
+        wanted = [[None] * SLOT for b in range(zs)]
+        for slot in range(SLOT):
+            spot = where_ref[(k * SOURCES + i) * SLOT + slot]
+            filled = jnp.where(spot < pattern_ref.shape[1], 1, 0)
+            spot = jnp.minimum(spot, pattern_ref.shape[1] - 1)
+            for b in range(zs):
+                wish = patterns[k, peer_z(-b), spot] * filled
+                wanted[b][slot] = wish.astype(jnp.float32).astype(keys.dtype)
 
         def half_scores(h, t):
             return jnp.dot(
@@ -304,11 +388,11 @@
             add_values(h, t, (scores + scores * jnp.tanh(scores)).astype(keys.dtype))
             scores = later
 
-        @pl.when((n == SOURCES - 1) & (k == 0))
-        def _():
-            own[...] = acc[...]
-
-        @pl.when((n == SOURCES - 1) & (k != 0))
+        @pl.when(ends & (k == 0))
+        def _():
+            own[...] += acc[...]
+
+        @pl.when(ends & (k != 0))
         def _():
             sums[k - 1] = acc[...].astype(sums.dtype)
             o_copy(k).start()
@@ -323,12 +407,13 @@
 
     for k in ORDER[1:]:
         o_copy(k).wait_recv()
-        if k != ORDER[3]:
-            own[...] += sums_in[k - 1].astype(jnp.float32)
     mine = None
     for i in HOPS + (0,):
         cols = slice(i * rows, (i + 1) * rows)
-        total = (own[:, cols] + sums_in[ORDER[3] - 1, :, cols].astype(jnp.float32)).T
+        total = own[:, cols]
+        for k in ORDER[1:]:
+            total += sums_in[k - 1, :, cols].astype(jnp.float32)
+        total = total.T
         if i == 0:
             mine = total
         else:
@@ -350,8 +435,6 @@
     out_ref[...] = total.astype(out_ref.dtype)
 
     for d in HOPS:
-        z1_copy(d).wait_send()
-        z2_copy(d).wait_send()
         z3_copy(d).wait_send()
         q_copy(d).wait_send()
         o_copy(d).wait_send()
@@ -363,14 +446,14 @@
     lax.fori_loop(0, (SOURCES - 1) * RING, drain, 0)
 
 
-def layer(zs, send, mask, ids, kv, table, w_query, w_gate, norm_gain, w_out):
+def layer(zs, send, where, ids, pattern, norm_gain, kv, table, w_query, w_gate, w_out):
     smem = pl.BlockSpec(memory_space=pltpu.SMEM)
     vmem = pl.BlockSpec(memory_space=pltpu.VMEM)
     hbm = pl.BlockSpec(memory_space=pl.ANY)
-    cands = ids.shape[0]
+    cands = ids.shape[1]
     rows = cands // zs
     width = table.shape[1]
-    part = w_query.shape[0]
+    part = w_query.shape[1]
     heads = part // DH
     kind = kv.dtype
     dma = pltpu.SemaphoreType.DMA
@@ -378,13 +461,22 @@
     return pl.pallas_call(
         functools.partial(layer_kernel, zs),
         out_shape=[jax.ShapeDtypeStruct(moved, kind), jax.ShapeDtypeStruct((rows, width), kind)],
-        in_specs=[smem, smem] + [vmem] * 7,
+        in_specs=[smem, smem, vmem, vmem, vmem] + [hbm] * 5,
         out_specs=[hbm, vmem],
         scratch_shapes=[
+            pltpu.VMEM(kv.shape, kind),
+            pltpu.VMEM(table.shape, kind),
+            pltpu.VMEM(w_query.shape, kind),
+            pltpu.VMEM(w_gate.shape, kind),
+            pltpu.VMEM(w_out.shape, kind),
+            pltpu.VMEM(w_query.shape[::-1], kind),
+            pltpu.VMEM((RING - 1,) + pattern.shape, pattern.dtype),
+            pltpu.SMEM((RING,) + pattern.shape, pattern.dtype),
             pltpu.VMEM(moved, kind),
             pltpu.VMEM((kv.shape[1], kv.shape[1]), kind),
             pltpu.VMEM((zs, rows, width), kind),
-            pltpu.VMEM((zs - 1, rows, width), kind),
+            pltpu.VMEM((2, rows // 2, width), kind),
+            pltpu.VMEM((2, rows, width), kind),
             pltpu.VMEM((zs, rows, width), kind),
             pltpu.VMEM((RING, part, cands), kind),
             pltpu.VMEM((rows, width), jnp.float32),
@@ -396,12 +488,16 @@
             pltpu.VMEM((RING - 1, part, cands), kind),
             pltpu.VMEM((zs, rows, part), kind),
             pltpu.VMEM((zs - 1, rows, part), kind),
+            dma((5,)),
+            dma((RING - 1,)),
+            dma((RING - 1,)),
+            dma((RING,)),
             dma((SOURCES * RING,)),
             dma((SOURCES * RING,)),
-            dma((zs - 1,)),
-            dma((zs - 1,)),
-            dma((zs - 1,)),
-            dma((zs - 1,)),
+            dma((6,)),
+            dma((6,)),
+            dma((6,)),
+            dma((6,)),
             dma((RING - 1,)),
             dma((RING - 1,)),
             dma((2,)),
@@ -411,60 +507,44 @@
             dma((zs - 1,)),
         ],
         compiler_params=pltpu.CompilerParams(
-            collective_id=0, has_side_effects=True, vmem_limit_bytes=60 * 2**20
+            collective_id=0, has_side_effects=True, vmem_limit_bytes=62 * 2**20
         ),
         name="layer",
-    )(send, mask, ids, kv, table, w_query, w_gate, norm_gain, w_out)[1]
+    )(send, where, ids, pattern, norm_gain, kv, table, w_query, w_gate, w_out)[1]
 
 
 def on_device(
     cand_items, item_table, kv_cache, hist_blocks, pattern, w_query, w_gate, norm_gain, w_out
 ):
     zs = lax.axis_size("item")
-    z = lax.axis_index("item")
     me = lax.axis_index("cache")
     blocks_here = kv_cache.shape[0]
     list_len = hist_blocks.shape[1]
-    item_ids = cand_items[0]
-    rows_per = item_ids.shape[0] // zs
-
     owner_of = hist_blocks // blocks_here
-    local_of = hist_blocks % blocks_here
-    same_owner = owner_of[:, :, None] == owner_of[:, None, :]
     positions = jnp.arange(list_len)
-    earlier = positions[None, :] < positions[:, None]
-    slot_rank = jnp.sum(same_owner & earlier[None], axis=2)
+    so_far = positions[None, :] <= positions[:, None]
     slots = jnp.arange(SLOT)
-    selected = (owner_of == me)[:, None, :] & (slot_rank[:, None, :] == slots[None, :, None])
-    send = jnp.sum(jnp.where(selected, local_of[:, None, :], 0), axis=2)
-
-    turned = lax.dynamic_slice_in_dim(
-        jnp.concatenate([item_ids, item_ids]), z * rows_per, item_ids.shape[0], 0
-    )
-    local_ids = (turned - z * item_table.shape[0])[:, None]
-    kv_rows = kv_cache.reshape(blocks_here, -1, kv_cache.shape[3])
+    mine = owner_of == me
+    count = jnp.sum((mine[:, None, :] & so_far[None]).astype(jnp.int32), axis=2)
+    chosen = mine[:, None, :] & (count[:, None, :] == slots[None, :, None] + 1)
+    send = jnp.sum(jnp.where(chosen, hist_blocks[:, None, :] - me * blocks_here, 0), axis=2)
 
     request = jnp.stack([ring_peer(k) for k in range(RING)])
     owner_idx = jnp.stack([kv_source(i) for i in range(SOURCES)])
-    rotation = (z - jnp.arange(zs)) % zs
-    pattern_of = [pattern[0]] + [
-        lax.ppermute(pattern[0], "cache", ring_pairs(-k)) for k in range(1, RING)
-    ]
-    pattern_k = jnp.stack(pattern_of)[:, rotation]
-    from_source = owner_of[request][:, None, None, :] == owner_idx[None, :, None, None]
-    in_slot = slot_rank[request][:, None, None, :] == slots[None, None, :, None]
-    filled = from_source & in_slot
-    mask = jnp.any(filled[:, :, None] & (pattern_k != 0)[:, None, :, None], axis=4)
+    held = owner_of[request][:, None, :] == owner_idx[None, :, None]
+    count = jnp.sum((held[:, :, None, :] & so_far[None, None]).astype(jnp.int32), axis=3)
+    where = jnp.sum((count[:, :, None, :] <= slots[None, None, :, None]).astype(jnp.int32), axis=3)
     out = layer(
         zs,
-        send.reshape(-1).astype(jnp.int32),
-        mask.reshape(-1).astype(jnp.float32),
-        local_ids,
-        kv_rows,
+        send.reshape(-1),
+        where.reshape(-1),
+        cand_items,
+        pattern[0],
+        norm_gain[None, :],
+        kv_cache.reshape(blocks_here, -1, kv_cache.shape[3]),
         item_table,
-        w_query.T,
+        w_query,
         w_gate,
-        norm_gain[None, :],
         w_out,
     )
     return out[None]

time: 202 us -> 162 us (0.80)
  Pallas kernels: 181 us -> 154 us
  starting transfers between devices: 5.74 us -> 0 us
  local copies, waits for them, and re-layouts: 8.4 us -> 3.94 us
  other arithmetic: 5.51 us -> 3.44 us
    pallas_call x1, Pallas kernels: 181 us -> 154 us  [layer(): pl.pallas_call(functools.partial(layer_kernel, zs), out_shape=[jax.ShapeD...]
    ppermute x3 -> x0, starting transfers between devices: 5.74 us -> none  [on_device(): lax.ppermute(pattern[0], 'cache', ring_pairs(-k))]
    unnamed x2 -> x1, local copies, waits for them, and re-layouts: 3.91 us -> 1.87 us
  transfers between devices with their start and end apart: 3 -> 0, of which waited for: 0 -> 0; matrix products, arithmetic and copies ran while one was open for 4% -> 0% of each run, Pallas kernels for 0% -> 0%
where the time goes in v4:
time: 162 us
  Pallas kernels  154 us (95%)
  local copies, waits for them, and re-layouts  3.94 us (2%)
  other arithmetic  3.44 us (2%)
    pallas_call x1, Pallas kernels, layer(): pl.pallas_call(functools.partial(layer_kernel, zs), out_shape=[jax.ShapeD...  154 us

profile of v4, /device:TPU:0, one launch (start us, length us, event | category | flops | bytes accessed | tf_op | source)
XLA Modules:
  0.0 161.6 jit_solution(942581700019591310)
XLA Ops:
  0.0 0.1 stack.55
  0.1 0.1 fusion.2
  0.2 0.7 broadcast_subtract_fusion
  0.9 0.7 broadcast_compare_fusion.1
  1.7 0.6 gather_fusion
  2.2 0.1 broadcast_compare_fusion
  2.3 0.6 convert_reduce_fusion
  2.9 0.4 convert_reduce_fusion.2
  3.3 0.1 copy.11
  3.4 0.6 reshape.208.where_ref
  4.0 0.6 convert_reduce_fusion.1
  4.6 0.2 select_reduce_fusion
  4.8 0.1 copy.10
  4.9 0.6 reshape.207.send_ref
  5.6 154.2 %layer.1 = (bf16[8,4,4,512,128]{4,3,2,1,0:T(8,128)(2,1)}, bf16[256,1024]{1,0:T(8,128)(2,1)}) custom-call(s32[128]{0:T(128)} %reshape.207.send_ref, s32[128]{0:T(128)} %reshape.208.where_ref, s32[1,1024]{1,0:T(1,128)} %ids_ref.1, s32[4,64]{1,0:T(4,128)} %bitcast.21, f32[1,1024]{1,0:T(1,128)} %bitcast.20, bf16[64,512,128]{2,1,0:T(8,128)(2,1)} %bitcast.18, ...), custom_call_target="tpu_custom_call" | custom-call | tf_op jit(solution)/shard_map/layer/pallas_call | solution.py:461
  159.8 1.9 %copy.13 = bf16[1,256,1024]{2,1,0:T(8,128)(2,1)} copy(bf16[1,256,1024]{2,1,0:T(8,128)(2,1)} %bitcast.19) | data formatting | bytes 1048576
  (3 shorter events, 0.0 us)

commit v5 on v4

--- a/solution.py
+++ b/solution.py
@@ -13,6 +13,7 @@
 RING = 4
 SOURCES = 8
 STEP = 256
+AHEAD = 17
 HOPS = (2, 1, 3)
 ORDER = (0, 2, 1, 3)
 
@@ -60,12 +61,12 @@
 
 
 def layer_kernel(
-    zs, send_ref, where_ref, ids_ref, pattern_ref, gain_ref, kv_hbm, table_hbm, wq_hbm, wg_hbm, wo_hbm,
+    zs, hist_ref, ids_ref, pattern_ref, gain_ref, kv_hbm, table_hbm, wq_hbm, wg_hbm, wo_hbm,
     recv_ref, out_ref,
-    kv_ref, table_ref, wq_ref, wg_ref, wo_ref, wq_turned, pattern_in, patterns,
+    kv_ref, table_ref, wq_ref, wg_ref, wo_ref, wq_turned, pattern_in, patterns, plan, tables,
     stage, turn, parts, relay_in, parts_in, chunks, queries, gate, held, keys, acc, own, sums, sums_in,
     pieces, pieces_in,
-    load_sem, pat_out, pat_in, pat_here, kv_out, kv_in, z1_out, z1_in, z2_out, z2_in, q_out, q_in, held_sem,
+    load_sem, plan_sem, pat_out, pat_in, pat_here, kv_out, kv_in, z1_out, z1_in, z2_out, z2_in, q_out, q_in, held_sem,
     o_out, o_in, z3_out, z3_in,
 ):
     z = lax.axis_index("item")
@@ -78,11 +79,50 @@
     loads = [
         pltpu.make_async_copy(src, dst, load_sem.at[n])
         for n, (src, dst) in enumerate(
-            [(table_hbm, table_ref), (kv_hbm, kv_ref), (wq_hbm, wq_ref), (wg_hbm, wg_ref), (wo_hbm, wo_ref)]
+            [(kv_hbm, kv_ref), (table_hbm, table_ref), (wq_hbm, wq_ref), (wg_hbm, wg_ref), (wo_hbm, wo_ref)]
         )
     ]
     for load in loads:
         load.start()
+
+    listed = hist_ref[...]
+    held_here = kv_hbm.shape[0]
+    length = listed.shape[1]
+    up_to = lax.broadcasted_iota(jnp.int32, (length, length), 0) <= lax.broadcasted_iota(
+        jnp.int32, (length, length), 1
+    )
+    up_to = jnp.where(up_to, 1.0, 0.0)
+    lane = lax.broadcasted_iota(jnp.int32, (SOURCES, plan.shape[2]), 1)
+    row = lax.broadcasted_iota(jnp.int32, (SOURCES, 1), 0)
+    me = lax.axis_index("cache")
+
+    def count(found):
+        return jnp.dot(jnp.where(found, 1.0, 0.0), up_to, preferred_element_type=jnp.float32)
+
+    for g in range(listed.shape[0] // SOURCES):
+        at_rows = slice(g * SOURCES, (g + 1) * SOURCES)
+        some = listed[at_rows]
+        found = lax.div(some, held_here) == me
+        nth = count(found)
+        table = jnp.zeros(lane.shape, jnp.int32)
+        for slot in range(SLOT):
+            block = jnp.where(found & (nth == slot + 1.0), some - me * held_here, 0)
+            table = jnp.where(lane == slot, jnp.sum(block, axis=1, keepdims=True), table)
+        plan[0, at_rows, :] = table
+    source = jnp.zeros(row.shape, jnp.int32)
+    for i in range(SOURCES):
+        source = jnp.where(row == i, kv_source(i), source)
+    for k in range(RING):
+        request = me if k == 0 else ring_peer(k)
+        some = jnp.broadcast_to(hist_ref[pl.ds(request, 1), :], (SOURCES, length))
+        nth = count(lax.div(some, held_here) == source)
+        table = jnp.zeros(lane.shape, jnp.int32)
+        for slot in range(SLOT):
+            spot = jnp.sum(jnp.where(nth <= slot, 1, 0), axis=1, keepdims=True)
+            table = jnp.where(lane == slot, spot, table)
+        plan[1, k * SOURCES : (k + 1) * SOURCES, :] = table
+    plan_copy = pltpu.make_async_copy(plan, tables, plan_sem.at[0])
+    plan_copy.start()
 
     barrier = pltpu.get_barrier_semaphore()
     for i in range(1, SOURCES):
@@ -111,34 +151,53 @@
     def own_copy(k):
         return pltpu.make_async_copy(stage.at[0, k], recv_ref.at[0, k], kv_out.at[k])
 
-    def send_blocks(k, first, last):
-        def step(n, carry):
-            i = source_at(n)
-            request = kv_request(i, k)
-            for slot in range(SLOT):
-                block = kv_ref[send_ref[request * SLOT + slot]]
-                by_head = jnp.dot(turn[...], block, preferred_element_type=jnp.float32)
-                turned = by_head.T.astype(stage.dtype)
-                by_head = by_head.astype(stage.dtype)
-                for p in range(heads // 2):
-                    stage[i, k, slot, p * BLK : (p + 1) * BLK, :] = jnp.concatenate(
-                        [by_head[h * BLK : (h + 1) * BLK, :DH] for h in (2 * p, 2 * p + 1)], axis=1
-                    )
-                for h in range(heads):
-                    first = heads // 2 * BLK + h * DH
-                    stage[i, k, slot, first : first + DH, :] = turned[DH:, h * BLK : (h + 1) * BLK]
-
-            @pl.when(i == 0)
-            def _():
-                own_copy(k).start()
-
-            @pl.when(i != 0)
-            def _():
-                kv_copy(i, k).start()
-
+    lead = SOURCES // 2
+
+    def unit(u):
+        group = lax.div(u + SOURCES - lead, SOURCES)
+        k = jnp.where(group == 1, ORDER[1], jnp.where(group == 2, ORDER[2], ORDER[3]))
+        k = jnp.where((group == 0) | (group == RING), 0, k)
+        n = lax.rem(u + SOURCES - lead, SOURCES)
+        n = jnp.where(group == 0, u, jnp.where(group == RING, u - (RING - 1) * SOURCES, n))
+        return source_at(n), k
+
+    def stage_unit(u):
+        i, k = unit(u)
+        request = kv_request(i, k)
+        for slot in range(SLOT):
+            block = kv_ref[tables[0, request, slot]]
+            by_head = jnp.dot(turn[...], block, preferred_element_type=jnp.float32)
+            turned = by_head.T.astype(stage.dtype)
+            by_head = by_head.astype(stage.dtype)
+            for p in range(heads // 2):
+                stage[i, k, slot, p * BLK : (p + 1) * BLK, :] = jnp.concatenate(
+                    [by_head[h * BLK : (h + 1) * BLK, :DH] for h in (2 * p, 2 * p + 1)], axis=1
+                )
+            for h in range(heads):
+                first = heads // 2 * BLK + h * DH
+                stage[i, k, slot, first : first + DH, :] = turned[DH:, h * BLK : (h + 1) * BLK]
+
+    def send_unit(u):
+        i, k = unit(u)
+
+        @pl.when(i == 0)
+        def _():
+            own_copy(k).start()
+
+        @pl.when(i != 0)
+        def _():
+            kv_copy(i, k).start()
+
+    def each_unit(first, last, *does):
+        def step(u, carry):
+            for do in does:
+                do(u)
             return carry
 
         lax.fori_loop(first, last, step, 0)
+
+    def send_units(first, last):
+        each_unit(first, last, stage_unit, send_unit)
 
     halves = {1: pl.ds(0, half), -1: pl.ds(half, half)}
 
@@ -232,16 +291,20 @@
             preferred_element_type=jnp.float32,
         ).astype(parts.dtype)
 
+    plan_copy.wait()
     loads[0].wait()
+    send_units(0, 1)
+    loads[1].wait()
     pick(2)
     relay_copy(1).start()
     relay_copy(-1).start()
+    send_units(1, 2)
     pick(1)
     part_copy(1, -1).start()
+    send_units(2, 3)
     pick(3)
     part_copy(-1, 1).start()
-    loads[1].wait()
-    send_blocks(0, 0, SOURCES // 2)
+    send_units(3, 5)
     relay_copy(1).wait()
     parts[1, halves[1]] += relay_in[0]
     part_copy(1, 1).start()
@@ -249,7 +312,7 @@
     parts[3, halves[-1]] += relay_in[1]
     part_copy(-1, -1).start()
     pick(0)
-    send_blocks(2, 0, SOURCES)
+    send_units(5, 9)
     for way in (1, -1):
         for h in (1, -1):
             part_copy(way, h).wait()
@@ -278,18 +341,20 @@
     for way in (1, -1):
         chunk_copy(way, way).wait()
         pass_copy(way).start()
-    send_blocks(1, 0, SOURCES)
+    send_units(9, AHEAD)
+    each_unit(AHEAD, 20, stage_unit)
     for way in (1, -1):
         chunk_copy(way, -way).wait()
     make_queries(1)
     make_queries(3)
+    each_unit(20, 28, stage_unit)
     for way in (1, -1):
         pass_copy(way).wait()
     make_queries(2)
     for k in HOPS:
         q_copy(k).start()
-    send_blocks(3, 0, SOURCES)
-    send_blocks(0, SOURCES // 2, SOURCES)
+    each_unit(AHEAD, 28, send_unit)
+    send_units(28, 32)
     gate[...] = silu(jnp.dot(chunks[0], wg_ref[...], preferred_element_type=jnp.float32))
     for k in HOPS:
         pattern_copy(k).wait()
@@ -297,16 +362,6 @@
     for k in range(RING):
         pattern_here(k).wait()
 
-    lead = SOURCES // 2
-
-    def unit(u):
-        group = lax.div(u + SOURCES - lead, SOURCES)
-        k = jnp.where(group == 1, ORDER[1], jnp.where(group == 2, ORDER[2], ORDER[3]))
-        k = jnp.where((group == 0) | (group == RING), 0, k)
-        n = lax.rem(u + SOURCES - lead, SOURCES)
-        n = jnp.where(group == 0, u, jnp.where(group == RING, u - (RING - 1) * SOURCES, n))
-        return source_at(n), k
-
     def fetch(u):
         i, k = unit(u)
         return pltpu.make_async_copy(recv_ref.at[i, k], held.at[lax.rem(u, 2)], held_sem.at[lax.rem(u, 2)])
@@ -331,6 +386,7 @@
 
     def one_unit(u, carry):
         i, k = unit(u)
+
         n = lax.rem(u + SOURCES - lead, SOURCES)
         starts = (n == 0) | (u == 0)
         ends = (n == SOURCES - 1) | (u == units - 1)
@@ -356,7 +412,7 @@
                 keys[2 * p + 1, at_slot, :] = pair[:, DH:]
         wanted = [[None] * SLOT for b in range(zs)]
         for slot in range(SLOT):
-            spot = where_ref[(k * SOURCES + i) * SLOT + slot]
+            spot = tables[1, k * SOURCES + i, slot]
             filled = jnp.where(spot < pattern_ref.shape[1], 1, 0)
             spot = jnp.minimum(spot, pattern_ref.shape[1] - 1)
             for b in range(zs):
@@ -446,8 +502,7 @@
     lax.fori_loop(0, (SOURCES - 1) * RING, drain, 0)
 
 
-def layer(zs, send, where, ids, pattern, norm_gain, kv, table, w_query, w_gate, w_out):
-    smem = pl.BlockSpec(memory_space=pltpu.SMEM)
+def layer(zs, hist, ids, pattern, norm_gain, kv, table, w_query, w_gate, w_out):
     vmem = pl.BlockSpec(memory_space=pltpu.VMEM)
     hbm = pl.BlockSpec(memory_space=pl.ANY)
     cands = ids.shape[1]
@@ -461,7 +516,7 @@
     return pl.pallas_call(
         functools.partial(layer_kernel, zs),
         out_shape=[jax.ShapeDtypeStruct(moved, kind), jax.ShapeDtypeStruct((rows, width), kind)],
-        in_specs=[smem, smem, vmem, vmem, vmem] + [hbm] * 5,
+        in_specs=[vmem] * 4 + [hbm] * 5,
         out_specs=[hbm, vmem],
         scratch_shapes=[
             pltpu.VMEM(kv.shape, kind),
@@ -472,6 +527,8 @@
             pltpu.VMEM(w_query.shape[::-1], kind),
             pltpu.VMEM((RING - 1,) + pattern.shape, pattern.dtype),
             pltpu.SMEM((RING,) + pattern.shape, pattern.dtype),
+            pltpu.VMEM((2, RING * SOURCES, 128), jnp.int32),
+            pltpu.SMEM((2, RING * SOURCES, 128), jnp.int32),
             pltpu.VMEM(moved, kind),
             pltpu.VMEM((kv.shape[1], kv.shape[1]), kind),
             pltpu.VMEM((zs, rows, width), kind),
@@ -489,6 +546,7 @@
             pltpu.VMEM((zs, rows, part), kind),
             pltpu.VMEM((zs - 1, rows, part), kind),
             dma((5,)),
+            dma((1,)),
             dma((RING - 1,)),
             dma((RING - 1,)),
             dma((RING,)),
@@ -510,38 +568,20 @@
             collective_id=0, has_side_effects=True, vmem_limit_bytes=62 * 2**20
         ),
         name="layer",
-    )(send, where, ids, pattern, norm_gain, kv, table, w_query, w_gate, w_out)[1]
+    )(hist, ids, pattern, norm_gain, kv, table, w_query, w_gate, w_out)[1]
 
 
 def on_device(
     cand_items, item_table, kv_cache, hist_blocks, pattern, w_query, w_gate, norm_gain, w_out
 ):
     zs = lax.axis_size("item")
-    me = lax.axis_index("cache")
-    blocks_here = kv_cache.shape[0]
-    list_len = hist_blocks.shape[1]
-    owner_of = hist_blocks // blocks_here
-    positions = jnp.arange(list_len)
-    so_far = positions[None, :] <= positions[:, None]
-    slots = jnp.arange(SLOT)
-    mine = owner_of == me
-    count = jnp.sum((mine[:, None, :] & so_far[None]).astype(jnp.int32), axis=2)
-    chosen = mine[:, None, :] & (count[:, None, :] == slots[None, :, None] + 1)
-    send = jnp.sum(jnp.where(chosen, hist_blocks[:, None, :] - me * blocks_here, 0), axis=2)
-
-    request = jnp.stack([ring_peer(k) for k in range(RING)])
-    owner_idx = jnp.stack([kv_source(i) for i in range(SOURCES)])
-    held = owner_of[request][:, None, :] == owner_idx[None, :, None]
-    count = jnp.sum((held[:, :, None, :] & so_far[None, None]).astype(jnp.int32), axis=3)
-    where = jnp.sum((count[:, :, None, :] <= slots[None, None, :, None]).astype(jnp.int32), axis=3)
     out = layer(
         zs,
-        send.reshape(-1),
-        where.reshape(-1),
+        hist_blocks,
         cand_items,
         pattern[0],
         norm_gain[None, :],
-        kv_cache.reshape(blocks_here, -1, kv_cache.shape[3]),
+        kv_cache.reshape(kv_cache.shape[0], -1, kv_cache.shape[3]),
         item_table,
         w_query,
         w_gate,

time: 162 us -> 147 us (0.907)
  Pallas kernels: 154 us -> 145 us
  other arithmetic: 3.44 us -> 0 us
  local copies, waits for them, and re-layouts: 3.94 us -> 1.87 us
    pallas_call x1, Pallas kernels: 154 us -> 145 us  [layer(): pl.pallas_call(functools.partial(layer_kernel, zs), out_shape=[jax.ShapeD...]
    reduce_sum x4 -> x0, other arithmetic: 1.81 us -> none  [the longest x1 0.62 us: on_device(): jnp.sum((held[:, :, None, :] & so_far[None, None]).astype(jnp.int32), axi...]
where the time goes in v5:
time: 147 us
  Pallas kernels  145 us (99%)
  local copies, waits for them, and re-layouts  1.87 us (1%)
    pallas_call x1, Pallas kernels, layer(): pl.pallas_call(functools.partial(layer_kernel, zs), out_shape=[jax.ShapeD...  145 us

profile of v5, /device:TPU:0, one launch (start us, length us, event | category | flops | bytes accessed | tf_op | source)
XLA Modules:
  0.0 147.1 jit_solution(13261413665982530970)
XLA Ops:
  0.0 145.2 %layer.1 = (bf16[8,4,4,512,128]{4,3,2,1,0:T(8,128)(2,1)}, bf16[256,1024]{1,0:T(8,128)(2,1)}) custom-call(s32[32,64]{1,0:T(8,128)} %hist_ref.1, s32[1,1024]{1,0:T(1,128)} %ids_ref.1, s32[4,64]{1,0:T(4,128)} %bitcast.7, f32[1,1024]{1,0:T(1,128)} %bitcast.6, bf16[64,512,128]{2,1,0:T(8,128)(2,1)} %bitcast.4, bf16[2048,1024]{1,0:T(8,128)(2,1)} %table_hbm.1, ...), custom_call_target="tpu_custom_call" | custom-call | tf_op jit(solution)/shard_map/layer/pallas_call | solution.py:516
  145.2 1.9 %copy.11 = bf16[1,256,1024]{2,1,0:T(8,128)(2,1)} copy(bf16[1,256,1024]{2,1,0:T(8,128)(2,1)} %bitcast.5) | data formatting | bytes 1048576

commit v6 on v5

--- a/solution.py
+++ b/solution.py
@@ -57,7 +57,7 @@
 
 
 def source_at(n):
-    return jnp.where(n < 2, n + 2, jnp.where(n < 4, n + 4, jnp.where(n < 6, 5 - n, n - 2)))
+    return jnp.where(n < 4, 2 + lax.div(n, 2) + 4 * lax.rem(n, 2), jnp.where(n < 6, n, 7 - n))
 
 
 def layer_kernel(
@@ -75,6 +75,13 @@
     heads = part // DH
     half = rows // 2
     peer_z = lambda d: lax.rem(z + d + zs, zs)
+
+    barrier = pltpu.get_barrier_semaphore()
+    for i in range(1, SOURCES):
+        pl.semaphore_signal(barrier, inc=1, device_id={"cache": kv_source(i)}, device_id_type=MESH)
+    for k in HOPS:
+        pl.semaphore_signal(barrier, inc=1, device_id={"cache": ring_peer(k)}, device_id_type=MESH)
+        pl.semaphore_signal(barrier, inc=1, device_id={"item": peer_z(k)}, device_id_type=MESH)
 
     loads = [
         pltpu.make_async_copy(src, dst, load_sem.at[n])
@@ -124,14 +131,6 @@
     plan_copy = pltpu.make_async_copy(plan, tables, plan_sem.at[0])
     plan_copy.start()
 
-    barrier = pltpu.get_barrier_semaphore()
-    for i in range(1, SOURCES):
-        pl.semaphore_signal(barrier, inc=1, device_id={"cache": kv_source(i)}, device_id_type=MESH)
-    for k in HOPS:
-        pl.semaphore_signal(barrier, inc=1, device_id={"cache": ring_peer(k)}, device_id_type=MESH)
-        pl.semaphore_signal(barrier, inc=1, device_id={"item": peer_z(k)}, device_id_type=MESH)
-    pl.semaphore_wait(barrier, SOURCES - 1 + 2 * len(HOPS))
-
     to = lax.broadcasted_iota(jnp.int32, turn.shape, 0)
     of = lax.broadcasted_iota(jnp.int32, turn.shape, 1)
     turn[...] = jnp.where(
@@ -275,6 +274,8 @@
             device_id={"item": peer_z(-i)},
             device_id_type=MESH,
         )
+
+    pl.semaphore_wait(barrier, SOURCES - 1 + 2 * len(HOPS))
 
     for k in HOPS:
         pattern_copy(k).start()
@@ -475,14 +476,19 @@
         else:
             pieces[i] = total.astype(pieces.dtype)
             z3_copy(i).start()
-    for i in HOPS:
+    row_mean = jnp.sum(mine, axis=1, keepdims=True)
+    row_square = jnp.sum(mine * mine, axis=1, keepdims=True)
+    for i in (1, 3, 2):
         z3_copy(i).wait_recv()
-    attended = [mine] + [pieces_in[i - 1].astype(jnp.float32) for i in range(1, zs)]
-    row_mean = sum(jnp.sum(a, axis=1, keepdims=True) for a in attended) / width
-    row_square = sum(jnp.sum(a * a, axis=1, keepdims=True) for a in attended) / width
+        piece = pieces_in[i - 1].astype(jnp.float32)
+        row_mean += jnp.sum(piece, axis=1, keepdims=True)
+        row_square += jnp.sum(piece * piece, axis=1, keepdims=True)
+    row_mean /= width
+    row_square /= width
     norm = lax.rsqrt(row_square - row_mean * row_mean + norm_eps)
     total = chunks[0].astype(jnp.float32)
-    for i, a in enumerate(attended):
+    for i in range(zs):
+        a = mine if i == 0 else pieces_in[i - 1].astype(jnp.float32)
         cols = pl.ds(pl.multiple_of(peer_z(i) * part, part), part)
         hidden = (a - row_mean) * norm * gain_ref[:, cols] * gate[:, cols]
         total += jnp.dot(

time: 147 us -> 146 us (level)
  no operation moved by 1% of the time
where the time goes in v6:
time: 146 us
  Pallas kernels  144 us (99%)
  local copies, waits for them, and re-layouts  1.87 us (1%)
    pallas_call x1, Pallas kernels, layer(): pl.pallas_call(functools.partial(layer_kernel, zs), out_shape=[jax.ShapeD...  144 us

profile of v6, /device:TPU:0, one launch (start us, length us, event | category | flops | bytes accessed | tf_op | source)
XLA Modules:
  0.0 146.0 jit_solution(14948762793032753549)
XLA Ops:
  0.0 144.1 %layer.1 = (bf16[8,4,4,512,128]{4,3,2,1,0:T(8,128)(2,1)}, bf16[256,1024]{1,0:T(8,128)(2,1)}) custom-call(s32[32,64]{1,0:T(8,128)} %hist_ref.1, s32[1,1024]{1,0:T(1,128)} %ids_ref.1, s32[4,64]{1,0:T(4,128)} %bitcast.7, f32[1,1024]{1,0:T(1,128)} %bitcast.6, bf16[64,512,128]{2,1,0:T(8,128)(2,1)} %bitcast.4, bf16[2048,1024]{1,0:T(8,128)(2,1)} %table_hbm.1, ...), custom_call_target="tpu_custom_call" | custom-call | tf_op jit(solution)/shard_map/layer/pallas_call | solution.py:522
  144.1 1.9 %copy.11 = bf16[1,256,1024]{2,1,0:T(8,128)(2,1)} copy(bf16[1,256,1024]{2,1,0:T(8,128)(2,1)} %bitcast.5) | data formatting | bytes 1048576

commit v7 on v6

--- a/solution.py
+++ b/solution.py
@@ -245,12 +245,13 @@
         src = pattern_ref if k == 0 else pattern_in.at[k - 1]
         return pltpu.make_async_copy(src, patterns.at[k], pat_here.at[k])
 
-    def q_copy(k):
+    def q_copy(k, d):
+        cols = pl.ds(d * rows, rows)
         return pltpu.make_async_remote_copy(
-            src_ref=queries.at[0],
-            dst_ref=queries.at[k],
-            send_sem=q_out.at[k - 1],
-            recv_sem=q_in.at[k - 1],
+            src_ref=queries.at[0, :, cols],
+            dst_ref=queries.at[k, :, cols],
+            send_sem=q_out.at[d * (RING - 1) + k - 1],
+            recv_sem=q_in.at[d * (RING - 1) + k - 1],
             device_id={"cache": ring_peer(-k)},
             device_id_type=MESH,
         )
@@ -337,6 +338,8 @@
                 wq_turned[...], chunks[d], (((1,), (1,)), ((), ())), preferred_element_type=jnp.float32
             )
         ).astype(queries.dtype) * jnp.asarray(scale, queries.dtype)
+        for k in HOPS:
+            q_copy(k, d).start()
 
     make_queries(0)
     for way in (1, -1):
@@ -352,8 +355,6 @@
     for way in (1, -1):
         pass_copy(way).wait()
     make_queries(2)
-    for k in HOPS:
-        q_copy(k).start()
     each_unit(AHEAD, 28, send_unit)
     send_units(28, 32)
     gate[...] = silu(jnp.dot(chunks[0], wg_ref[...], preferred_element_type=jnp.float32))
@@ -403,7 +404,8 @@
 
             @pl.when(k != 0)
             def _():
-                q_copy(k).wait_recv()
+                for d in range(zs):
+                    q_copy(k, d).wait_recv()
 
         for slot in range(SLOT):
             at_slot = slice(slot * BLK, (slot + 1) * BLK)
@@ -498,7 +500,8 @@
 
     for d in HOPS:
         z3_copy(d).wait_send()
-        q_copy(d).wait_send()
+        for c in range(zs):
+            q_copy(d, c).wait_send()
         o_copy(d).wait_send()
 
     def drain(n, carry):
@@ -562,8 +565,8 @@
             dma((6,)),
             dma((6,)),
             dma((6,)),
-            dma((RING - 1,)),
-            dma((RING - 1,)),
+            dma((zs * (RING - 1),)),
+            dma((zs * (RING - 1),)),
             dma((2,)),
             dma((RING - 1,)),
             dma((RING - 1,)),

time: 146 us -> 153 us (1.048)
  Pallas kernels: 144 us -> 150 us
    pallas_call x1, Pallas kernels: 144 us -> 150 us  [layer(): pl.pallas_call(functools.partial(layer_kernel, zs), out_shape=[jax.ShapeD...]
where the time goes in v7:
time: 153 us; the launch traced here: 152 us
  Pallas kernels  150 us (98%)
  local copies, waits for them, and re-layouts  1.87 us (1%)
    pallas_call x1, Pallas kernels, layer(): pl.pallas_call(functools.partial(layer_kernel, zs), out_shape=[jax.ShapeD...  150 us

profile of v7, /device:TPU:0, one launch (start us, length us, event | category | flops | bytes accessed | tf_op | source)
XLA Modules:
  0.0 152.0 jit_solution(11347740431325501326)
XLA Ops:
  0.0 150.1 %layer.1 = (bf16[8,4,4,512,128]{4,3,2,1,0:T(8,128)(2,1)}, bf16[256,1024]{1,0:T(8,128)(2,1)}) custom-call(s32[32,64]{1,0:T(8,128)} %hist_ref.1, s32[1,1024]{1,0:T(1,128)} %ids_ref.1, s32[4,64]{1,0:T(4,128)} %bitcast.7, f32[1,1024]{1,0:T(1,128)} %bitcast.6, bf16[64,512,128]{2,1,0:T(8,128)(2,1)} %bitcast.4, bf16[2048,1024]{1,0:T(8,128)(2,1)} %table_hbm.1, ...), custom_call_target="tpu_custom_call" | custom-call | tf_op jit(solution)/shard_map/layer/pallas_call | solution.py:525
  150.1 1.9 %copy.11 = bf16[1,256,1024]{2,1,0:T(8,128)(2,1)} copy(bf16[1,256,1024]{2,1,0:T(8,128)(2,1)} %bitcast.5) | data formatting | bytes 1048576
